TPU v7x, 256 devices: a whole 4x4x8 slice. The times are simulated.
256 devices in a mesh: ctx: 64 (over y, x_lo, z), head: 4 (over x_hi, core).
Axes of the slice: x: 4 (x_hi: 2, x_lo: 2; x = x_hi * 2 + x_lo), y: 4, z: 8, core: 2. Of those that a mesh axis runs over, the one named last changes fastest.
Arguments:
- queries: bfloat16 [32768, 4, 512], P('ctx', 'head'), may hold values from -5 to 5
- keys: bfloat16 [32768, 512], P('ctx'), may hold values from -5 to 5
- values: bfloat16 [32768, 512], P('ctx'), may hold values from -5 to 5
- grad_out: bfloat16 [32768, 4, 512], P('ctx', 'head'), may hold values from -24 to 24
- doc_lengths: int32 [64], replicated, may hold values from 1 to 1024, 32768 in all
Outputs:
- query_grad: bfloat16 [32768, 4, 512], P('ctx', 'head')
- key_grad: bfloat16 [32768, 512], P(('ctx', 'head'))
- value_grad: bfloat16 [32768, 512], P(('ctx', 'head'))
Inputs may be any that keep to these rules, and one draw needn't show every extreme that they name: `doc_lengths`: documents packed one after another; the lengths sum to 32768 and the longest has exactly 1024 tokens.
All inputs are finite; a program needn't handle non-finite values.
Results may differ from a plain program's by a relative error of at most 0.011.
Values may be sent and summed in bfloat16 or wider, within the bound.
A program may use at most 64 MiB of HBM per device.

v0:
```python
import math

import jax
import jax.numpy as jnp
from jax import lax
from jax.sharding import PartitionSpec as P

HD = 128
KVH = 4
HOPS = 2


def shifted(value, axis, steps):
    count = lax.axis_size(axis)
    first, last = (max(0, -steps), min(count, count - steps))
    return lax.ppermute(value, axis, [(source, source + steps) for source in range(first, last)])


def doc_index(doc_ends, positions):
    return jnp.sum((doc_ends[None, :] <= positions[:, None]).astype(jnp.int32), axis=1)


def local(queries, keys, values, grad_out, doc_lengths):
    tok_rows = keys.shape[0]
    members = queries.shape[1]
    score_scale = 1.0 / math.sqrt(HD)
    ctx_place = lax.axis_index("ctx")
    doc_ends = jnp.cumsum(doc_lengths)
    offsets = jnp.arange(tok_rows, dtype=jnp.int32)
    q_pos = ctx_place * tok_rows + offsets
    q_doc = doc_index(doc_ends, q_pos)
    hop_masks = []
    for hop_index in range(HOPS + 1):
        k_pos = (ctx_place - hop_index) * tok_rows + offsets
        same_doc = doc_index(doc_ends, k_pos)[None, :] == q_doc[:, None]
        hop_masks.append((k_pos[None, :] <= q_pos[:, None]) & (k_pos[None, :] >= 0) & same_doc)
    q_heads = queries.reshape(tok_rows, members, KVH, HD)
    g_heads = grad_out.reshape(tok_rows, members, KVH, HD)
    home_block = jnp.stack([keys, values])
    blocks = [home_block]
    for hop_index in range(HOPS):
        blocks.append(shifted(blocks[-1], "ctx", 1))

    def scores_of(hop_index):
        k_part = blocks[hop_index][0].reshape(tok_rows, KVH, HD)
        raw_scores = (
            jnp.einsum("tmgd,ugd->mgtu", q_heads, k_part, preferred_element_type=jnp.float32)
            * score_scale
        )
        return jnp.where(hop_masks[hop_index][None, None], raw_scores, -jnp.inf)

    first_scores = scores_of(0)
    row_top = jnp.max(first_scores, axis=-1, keepdims=True)
    row_total = jnp.sum(jnp.exp(first_scores - row_top), axis=-1, keepdims=True)
    for hop_index in range(1, HOPS + 1):

        def widen(carried, hop_index=hop_index):
            old_top, old_total = carried
            raw_scores = scores_of(hop_index)
            new_top = jnp.maximum(old_top, jnp.max(raw_scores, axis=-1, keepdims=True))
            new_total = old_total * jnp.exp(old_top - new_top) + jnp.sum(
                jnp.exp(raw_scores - new_top), axis=-1, keepdims=True
            )
            return (new_top, new_total)

        row_top, row_total = widen((row_top, row_total))
    log_norm = row_top + jnp.log(row_total)

    def weights_of(hop_index):
        weights = jnp.exp(scores_of(hop_index) - log_norm)
        return (weights, weights.astype(jnp.bfloat16))

    attn_out = jnp.zeros((tok_rows, members, KVH, HD), jnp.float32)
    for hop_index in range(HOPS + 1):

        def add_values(carried, hop_index=hop_index):
            weights_b = weights_of(hop_index)[1]
            v_part = blocks[hop_index][1].reshape(tok_rows, KVH, HD)
            return carried + jnp.einsum(
                "mgtu,ugd->tmgd", weights_b, v_part, preferred_element_type=jnp.float32
            )

        attn_out = add_values(attn_out)
    row_delta = jnp.einsum("tmgd,tmgd->mgt", g_heads.astype(jnp.float32), attn_out)[..., None]
    query_grads = jnp.zeros((tok_rows, members, KVH, HD), jnp.float32)
    zeros_grad = jnp.zeros((2, tok_rows, KVH * HD), jnp.float32)
    partials = []
    for hop_index in range(HOPS + 1):

        def hop_grads(carried, hop_index=hop_index):
            weights, weights_b = weights_of(hop_index)
            k_part = blocks[hop_index][0].reshape(tok_rows, KVH, HD)
            v_part = blocks[hop_index][1].reshape(tok_rows, KVH, HD)
            weight_grads = jnp.einsum(
                "tmgd,ugd->mgtu", g_heads, v_part, preferred_element_type=jnp.float32
            )
            score_grads = (weights * (weight_grads - row_delta) * score_scale).astype(jnp.bfloat16)
            new_query = carried[0] + jnp.einsum(
                "mgtu,ugd->tmgd", score_grads, k_part, preferred_element_type=jnp.float32
            )
            key_part = jnp.einsum(
                "mgtu,tmgd->ugd", score_grads, q_heads, preferred_element_type=jnp.float32
            ).reshape(tok_rows, KVH * HD)
            value_part = jnp.einsum(
                "mgtu,tmgd->ugd", weights_b, g_heads, preferred_element_type=jnp.float32
            ).reshape(tok_rows, KVH * HD)
            return (new_query, jnp.stack([key_part, value_part]))

        query_grads, grad_pair = hop_grads((query_grads, zeros_grad))
        partials.append(grad_pair)
    returned = partials[HOPS]
    for hop_index in range(HOPS - 1, -1, -1):
        returned = partials[hop_index] + shifted(returned, "ctx", -1)
    returned = lax.psum_scatter(returned, "head", scatter_dimension=1, tiled=True)
    query_grad = query_grads.reshape(tok_rows, members, KVH * HD).astype(jnp.bfloat16)
    return (query_grad, returned[0].astype(jnp.bfloat16), returned[1].astype(jnp.bfloat16))


def solution(mesh):
    placed = (P("ctx", "head", None), P("ctx", None), P("ctx", None), P("ctx", "head", None), P())
    return jax.shard_map(
        local,
        mesh=mesh,
        in_specs=placed,
        out_specs=(P("ctx", "head", None), P(("ctx", "head"), None), P(("ctx", "head"), None)),
        check_vma=False,
    )
```

profile of v0, /device:TPU:1, one launch (start us, length us, event | category | flops | bytes accessed | tf_op | source)
XLA Modules:
  0.0 260.1 jit_solution(4860819260532187508)
XLA Ops:
  9.9 5.4 %collective-permute-start = (bf16[2,512,512]{1,2,0:T(8,128)(2,1)S(1)}, bf16[2,512,512]{1,2,0:T(8,128)(2,1)}, u32[]{:S(2)}, u32[]{:S(2)}) collective-permute-start(bf16[2,512,512]{1,2,0:T(8,128)(2,1)S(1)} %pad_maximum_fusion.1), channel_id=1, source_target_pairs={{0,4},{4,8},{8,12},{12,16},{16,20},{20,24},{24,28},{28,32},{32,36}... | collective-permute-start | bytes 3145736 | tf_op jit(solution)/shard_map/ppermute | solution.py:16
  17.3 18.8 %collective-permute-done = bf16[2,512,512]{1,2,0:T(8,128)(2,1)} collective-permute-done((bf16[2,512,512]{1,2,0:T(8,128)(2,1)S(1)}, bf16[2,512,512]{1,2,0:T(8,128)(2,1)}, u32[]{:S(2)}, u32[]{:S(2)}) %collective-permute-start) | collective-permute-done | bytes 1048608 | tf_op jit(solution)/shard_map/ppermute | solution.py:16
  36.1 5.2 %collective-permute-start.1 = (bf16[2,512,512]{1,2,0:T(8,128)(2,1)}, bf16[2,512,512]{1,2,0:T(8,128)(2,1)}, u32[]{:S(2)}, u32[]{:S(2)}) collective-permute-start(bf16[2,512,512]{1,2,0:T(8,128)(2,1)} %collective-permute-done), channel_id=1, source_target_pairs={{0,4},{4,8},{8,12},{12,16},{16,20},{20,24},{24,28},{28,32},{32,36}... | collective-permute-start | bytes 3145736 | tf_op jit(solution)/shard_map/ppermute | solution.py:16
  41.2 2.8 %fusion.9 = (f32[4,512]{1,0:T(4,128)S(1)}, f32[4,512,512]{2,1,0:T(8,128)}) fusion(pred[512,512]{0,1:T(8,128)(4,1)S(1)} %get-tuple-element.25, bf16[512,4,128]{0,2,1:T(8,128)(2,1)S(1)} %bitcast.206, bf16[512,4,128]{0,2,1:T(8,128)(2,1)S(1)} %bitcast.199), kind=kOutput, calls=%fused_computation.24 | convolution fusion | flops 271579136 | bytes 5513216 | tf_op jit(solution)/shard_map/tmgd,ugd->mgtu/dot_general | solution.py:47
  46.4 3.1 %exponential_reduce_fusion.2 = f32[4,512]{1,0:T(4,128)S(1)} fusion(f32[4,512,512]{2,1,0:T(8,128)} %get-tuple-element.29, f32[4,512]{1,0:T(4,128)S(1)} %get-tuple-element.28, pred[512,512]{0,1:T(8,128)(4,1)S(1)} %get-tuple-element.25), kind=kLoop, calls=%fused_computation.20 | loop fusion | flops 4192256 | bytes 4472832 | tf_op jit(solution)/shard_map/reduce_sum | solution.py:54
  49.5 2.1 fusion.55
  52.5 9.0 %collective-permute-done.1 = bf16[2,512,512]{1,2,0:T(8,128)(2,1)} collective-permute-done((bf16[2,512,512]{1,2,0:T(8,128)(2,1)}, bf16[2,512,512]{1,2,0:T(8,128)(2,1)}, u32[]{:S(2)}, u32[]{:S(2)}) %collective-permute-start.1) | collective-permute-done | bytes 1048608 | tf_op jit(solution)/shard_map/ppermute | solution.py:16
  61.5 2.1 fusion.54
  68.4 2.5 convolution_bitcast_fusion
  70.8 2.3 fusion.50
  73.1 2.6 copy.138
  75.7 4.0 %convolution_add_fusion.1 = f32[4,128,512]{1,2,0:T(8,128)S(1)} fusion(f32[4,128,512]{1,2,0:T(8,128)} %convolution_bitcast_fusion, bf16[512,4,128]{0,2,1:T(8,128)(2,1)S(1)} %bitcast.217, f32[4,512,512]{2,1,0:T(8,128)} %copy-done, f32[4,512]{1,0:T(4,128)S(1)} %log_add_fusion, pred[512,512]{0,1:T(8,128)(4,1)S(1)} %get-tuple-element.23), kind=kOutput, calls=%fused_computation.51 | convolution fusion | flops 272891904 | bytes 7086080 | tf_op jit(solution)/shard_map/mgtu,ugd->tmgd/dot_general | solution.py:79
  82.4 4.2 %fusion.1 = bf16[1,4,512,512]{2,3,1,0:T(8,128)(2,1)S(1)} fusion(f32[4,512,512]{2,1,0:T(8,128)} %copy-done.2, bf16[512,4,128]{0,2,1:T(8,128)(2,1)} %bitcast.219, bf16[512,4,128]{0,2,1:T(8,128)(2,1)} %copy.124, f32[4,512]{1,0:T(4,128)S(1)} %copy.153, f32[4,512]{1,0:T(4,128)S(1)} %log_add_fusion, pred[512,512]{0,1:T(8,128)(4,1)S(1)} %get-tuple-element.24), kind=kOutput, calls=%fused_computation.5 | convolution fusion | flops 275775488 | bytes 7618560 | tf_op jit(solution)/shard_map/tmgd,ugd->mgtu/dot_general | solution.py:94
  90.0 2.9 %pad_maximum_fusion = f32[2,512,512]{2,1,0:T(8,128)} fusion(f32[1,512,512]{2,1,0:T(8,128)S(1)} %copy-done.13, f32[1,512,512]{2,1,0:T(8,128)} %copy.137), kind=kLoop, calls=%fused_computation.32 | loop fusion | flops 524288 | bytes 4194304 | tf_op jit(solution)/shard_map/stack | solution.py:107
  94.3 3.3 %fusion.47 = f32[4,512,128]{1,2,0:T(8,128)} fusion(bf16[512,4,128]{0,2,1:T(8,128)(2,1)} %copy.124, f32[4,512,512]{2,1,0:T(8,128)S(1)} %copy-done.1, f32[4,512]{1,0:T(4,128)S(1)} %log_add_fusion, pred[512,512]{0,1:T(8,128)(4,1)S(1)} %get-tuple-element.23), kind=kOutput, calls=%fused_computation.75 | convolution fusion | flops 272629760 | bytes 6037504 | tf_op jit(solution)/shard_map/mgtu,tmgd->ugd/dot_general | solution.py:104
  99.2 3.8 %fusion.3 = bf16[1,4,512,512]{2,3,1,0:T(8,128)(2,1)S(1)} fusion(f32[4,512,512]{2,1,0:T(8,128)} %copy-done, bf16[512,4,128]{0,2,1:T(8,128)(2,1)S(1)} %bitcast.218, bf16[512,4,128]{0,2,1:T(8,128)(2,1)S(1)} %copy-done.22, f32[4,512]{1,0:T(4,128)S(1)} %copy.153, f32[4,512]{1,0:T(4,128)S(1)} %log_add_fusion, pred[512,512]{0,1:T(8,128)(4,1)S(1)} %get-tuple-element.23), kind=kOutput, calls=%fused_computation.9 | convolution fusion | flops 275775488 | bytes 7618560 | tf_op jit(solution)/shard_map/tmgd,ugd->mgtu/dot_general | solution.py:94
  106.5 34.4 %collective-permute-done.2 = f32[2,512,512]{2,1,0:T(8,128)} collective-permute-done((f32[2,512,512]{2,1,0:T(8,128)}, f32[2,512,512]{2,1,0:T(8,128)}, u32[]{:S(2)}, u32[]{:S(2)}) %collective-permute-start.2) | collective-permute-done | bytes 2097184 | tf_op jit(solution)/shard_map/ppermute | solution.py:16
  140.9 3.7 %maximum_add_fusion.1 = f32[2,512,512]{2,1,0:T(8,128)} fusion(f32[2,512,512]{2,1,0:T(8,128)} %collective-permute-done.2, f32[1,512,512]{2,1,0:T(8,128)S(1)} %copy.132, f32[1,512,512]{2,1,0:T(8,128)} %copy.131), kind=kLoop, calls=%fused_computation.31 | loop fusion | flops 1048576 | bytes 6291456 | tf_op jit(solution)/shard_map/add | solution.py:113
  148.8 4.0 %fusion.5 = bf16[1,4,512,512]{2,3,1,0:T(8,128)(2,1)S(1)} fusion(f32[4,512,512]{2,1,0:T(8,128)} %get-tuple-element.29, bf16[512,4,128]{0,2,1:T(8,128)(2,1)} %copy.124, f32[4,512]{1,0:T(4,128)S(1)} %copy.153, f32[4,512]{1,0:T(4,128)S(1)} %log_add_fusion, pred[512,512]{0,1:T(8,128)(4,1)S(1)} %copy-done.15, bf16[512,512]{1,0:T(8,128)(2,1)} %param.7), kind=kOutput, calls=%fused_computation.13 | convolution fusion | flops 275775488 | bytes 7618560 | tf_op jit(solution)/shard_map/tmgd,ugd->mgtu/dot_general | solution.py:94
  154.6 2.5 copy.125
  157.1 33.8 %collective-permute-done.3 = f32[2,512,512]{2,1,0:T(8,128)} collective-permute-done((f32[2,512,512]{2,1,0:T(8,128)}, f32[2,512,512]{2,1,0:T(8,128)}, u32[]{:S(2)}, u32[]{:S(2)}) %collective-permute-start.3) | collective-permute-done | bytes 2097184 | tf_op jit(solution)/shard_map/ppermute | solution.py:16
  190.9 4.0 %maximum_add_fusion = f32[2,512,512]{2,1,0:T(8,128)} fusion(f32[2,512,512]{2,1,0:T(8,128)} %collective-permute-done.3, f32[1,512,512]{2,1,0:T(8,128)} %copy.126, f32[1,512,512]{2,1,0:T(8,128)} %copy.125), kind=kLoop, calls=%fused_computation.30 | loop fusion | flops 1048576 | bytes 6291456 | tf_op jit(solution)/shard_map/add | solution.py:113
  196.0 2.0 fusion.30
  199.5 52.0 %reduce-scatter.2.cloned.1.call-done = f32[2,128,512]{2,1,0:T(8,128)} async-done(((f32[2,512,512]{2,1,0:T(8,128)}), f32[2,128,512]{2,1,0:T(8,128)}) %reduce-scatter.2.cloned.1.call-update) | async-done | bytes 524304 | tf_op jit(solution)/shard_map/reduce_scatter | solution.py:114
  (91 shorter events, 35.2 us)
Async XLA Ops:
  7.2 8.2 %copy-start.24 = (s32[64]{0:T(128)S(1)}, s32[64]{0:T(128)}, u32[]{:S(2)}) copy-start(s32[64]{0:T(128)} %param.9) | copy-start | bytes 772
  7.2 8.5 %copy-start.19 = (bf16[512,1,512]{2,0,1:T(8,128)(2,1)S(1)}, bf16[512,1,512]{2,0,1:T(8,128)(2,1)}, u32[]{:S(2)}) copy-start(bf16[512,1,512]{2,0,1:T(8,128)(2,1)} %param.5) | copy-start | bytes 1572868
  7.2 244.3 %reduce-scatter.2.cloned.1.call-start = ((), (), s32[]{:S(2)}) async-start(), calls=%async_computation.1 | async-start | bytes 2621440 | tf_op jit(solution)/shard_map/reduce_scatter | solution.py:114
  9.9 26.2 %collective-permute-start = (bf16[2,512,512]{1,2,0:T(8,128)(2,1)S(1)}, bf16[2,512,512]{1,2,0:T(8,128)(2,1)}, u32[]{:S(2)}, u32[]{:S(2)}) collective-permute-start(bf16[2,512,512]{1,2,0:T(8,128)(2,1)S(1)} %pad_maximum_fusion.1), channel_id=1, source_target_pairs={{0,4},{4,8},{8,12},{12,16},{16,20},{20,24},{24,28},{28,32},{32,36}... | collective-permute-start | bytes 3145736 | tf_op jit(solution)/shard_map/ppermute | solution.py:16
  17.3 49.2 %copy-start.14 = (pred[512,512]{0,1:T(8,128)(4,1)}, pred[512,512]{0,1:T(8,128)(4,1)S(1)}, u32[]{:S(2)}) copy-start(pred[512,512]{0,1:T(8,128)(4,1)S(1)} %get-tuple-element.25) | copy-start | bytes 786436
  36.1 25.4 %collective-permute-start.1 = (bf16[2,512,512]{1,2,0:T(8,128)(2,1)}, bf16[2,512,512]{1,2,0:T(8,128)(2,1)}, u32[]{:S(2)}, u32[]{:S(2)}) collective-permute-start(bf16[2,512,512]{1,2,0:T(8,128)(2,1)} %collective-permute-done), channel_id=1, source_target_pairs={{0,4},{4,8},{8,12},{12,16},{16,20},{20,24},{24,28},{28,32},{32,36}... | collective-permute-start | bytes 3145736 | tf_op jit(solution)/shard_map/ppermute | solution.py:16
  51.5 13.0 %copy-start.9 = (bf16[1,512,512]{1,2,0:T(8,128)(2,1)}, bf16[1,512,512]{1,2,0:T(8,128)(2,1)S(1)}, u32[]{:S(2)}) copy-start(bf16[1,512,512]{1,2,0:T(8,128)(2,1)S(1)} %get-tuple-element.20) | copy-start | bytes 1572868
  52.5 13.0 %copy-start = (f32[4,512,512]{2,1,0:T(8,128)}, f32[4,512,512]{2,1,0:T(8,128)S(1)}, u32[]{:S(2)}) copy-start(f32[4,512,512]{2,1,0:T(8,128)S(1)} %get-tuple-element.31) | copy-start | bytes 12582916
  64.5 6.3 %copy-start.2 = (f32[4,512,512]{2,1,0:T(8,128)}, f32[4,512,512]{2,1,0:T(8,128)S(1)}, u32[]{:S(2)}) copy-start(f32[4,512,512]{2,1,0:T(8,128)S(1)} %get-tuple-element.27) | copy-start | bytes 12582916
  64.5 3.7 %copy-start.4 = (f32[4,512,512]{2,1,0:T(8,128)S(1)}, f32[4,512,512]{2,1,0:T(8,128)}, u32[]{:S(2)}) copy-start(f32[4,512,512]{2,1,0:T(8,128)} %get-tuple-element.29) | copy-start | bytes 12582916
  64.6 3.8 %copy-start.20 = (bf16[512,512]{1,0:T(8,128)(2,1)S(1)}, bf16[512,512]{1,0:T(8,128)(2,1)}, u32[]{:S(2)}) copy-start(bf16[512,512]{1,0:T(8,128)(2,1)} %param.7) | copy-start | bytes 1572868
  66.4 4.4 %copy-start.21 = (bf16[512,4,128]{0,2,1:T(8,128)(2,1)S(1)}, bf16[512,4,128]{0,2,1:T(8,128)(2,1)}, u32[]{:S(2)}) copy-start(bf16[512,4,128]{0,2,1:T(8,128)(2,1)} %copy.124) | copy-start | bytes 1572868
  70.8 4.9 %copy-start.16 = (bf16[1,512,512]{1,2,0:T(8,128)(2,1)S(1)}, bf16[1,512,512]{1,2,0:T(8,128)(2,1)}, u32[]{:S(2)}) copy-start(bf16[1,512,512]{1,2,0:T(8,128)(2,1)} %get-tuple-element.19) | copy-start | bytes 1572868
  75.7 4.0 %copy-start.3 = (f32[4,512,512]{2,1,0:T(8,128)S(1)}, f32[4,512,512]{2,1,0:T(8,128)}, u32[]{:S(2)}) copy-start(f32[4,512,512]{2,1,0:T(8,128)} %copy-done.2) | copy-start | bytes 12582916
  75.7 4.0 %copy-start.18 = (bf16[1,512,512]{1,2,0:T(8,128)(2,1)S(1)}, bf16[1,512,512]{1,2,0:T(8,128)(2,1)}, u32[]{:S(2)}) copy-start(bf16[1,512,512]{1,2,0:T(8,128)(2,1)} %get-tuple-element.17) | copy-start | bytes 1572868
  90.0 4.3 %copy-start.1 = (f32[4,512,512]{2,1,0:T(8,128)S(1)}, f32[4,512,512]{2,1,0:T(8,128)}, u32[]{:S(2)}) copy-start(f32[4,512,512]{2,1,0:T(8,128)} %copy-done) | copy-start | bytes 12582916
  92.9 6.3 %copy-start.17 = (bf16[1,512,512]{1,2,0:T(8,128)(2,1)S(1)}, bf16[1,512,512]{1,2,0:T(8,128)(2,1)}, u32[]{:S(2)}) copy-start(bf16[1,512,512]{1,2,0:T(8,128)(2,1)} %get-tuple-element.19) | copy-start | bytes 1572868
  92.9 6.3 %copy-start.22 = (bf16[512,4,128]{0,2,1:T(8,128)(2,1)S(1)}, bf16[512,4,128]{0,2,1:T(8,128)(2,1)}, u32[]{:S(2)}) copy-start(bf16[512,4,128]{0,2,1:T(8,128)(2,1)} %copy.124) | copy-start | bytes 1572868
  92.9 48.0 %collective-permute-start.2 = (f32[2,512,512]{2,1,0:T(8,128)}, f32[2,512,512]{2,1,0:T(8,128)}, u32[]{:S(2)}, u32[]{:S(2)}) collective-permute-start(f32[2,512,512]{2,1,0:T(8,128)} %pad_maximum_fusion), channel_id=1, source_target_pairs={{4,0},{8,4},{12,8},{16,12},{20,16},{24,20},{28,24},{32,28},{36,32}... | collective-permute-start | bytes 6291464 | tf_op jit(solution)/shard_map/ppermute | solution.py:16
  105.2 40.9 %copy-start.15 = (pred[512,512]{0,1:T(8,128)(4,1)S(1)}, pred[512,512]{0,1:T(8,128)(4,1)}, u32[]{:S(2)}) copy-start(pred[512,512]{0,1:T(8,128)(4,1)} %copy-done.14) | copy-start | bytes 786436
  106.5 39.6 %copy-start.5 = (f32[4,512,512]{2,1,0:T(8,128)S(1)}, f32[4,512,512]{2,1,0:T(8,128)}, u32[]{:S(2)}) copy-start(f32[4,512,512]{2,1,0:T(8,128)} %get-tuple-element.29) | copy-start | bytes 12582916
  106.5 39.6 %copy-start.23 = (bf16[512,4,128]{0,2,1:T(8,128)(2,1)S(1)}, bf16[512,4,128]{0,2,1:T(8,128)(2,1)}, u32[]{:S(2)}) copy-start(bf16[512,4,128]{0,2,1:T(8,128)(2,1)} %copy.124) | copy-start | bytes 1572868
  144.6 46.3 %collective-permute-start.3 = (f32[2,512,512]{2,1,0:T(8,128)}, f32[2,512,512]{2,1,0:T(8,128)}, u32[]{:S(2)}, u32[]{:S(2)}) collective-permute-start(f32[2,512,512]{2,1,0:T(8,128)} %maximum_add_fusion.1), channel_id=1, source_target_pairs={{4,0},{8,4},{12,8},{16,12},{20,16},{24,20},{28,24},{32,28},{36,32}... | collective-permute-start | bytes 6291464 | tf_op jit(solution)/shard_map/ppermute | solution.py:16
  194.9 3.1 %copy-start.7 = (bf16[1,4,512,512]{2,3,1,0:T(8,128)(2,1)S(1)}, bf16[1,4,512,512]{2,3,1,0:T(8,128)(2,1)}, u32[]{:S(2)}) copy-start(bf16[1,4,512,512]{2,3,1,0:T(8,128)(2,1)} %copy-done.6) | copy-start | bytes 6291460
  (6 other events, 10.8 us)
Sparse Core Ops, SparseCore 0:
  195.1 56.3 reduce-scatter.1
where the time goes:
time: 261 us; the launch traced here: 260 us
  waiting for transfers between devices  148 us (57%)
  matrix products  37.8 us (14%)
  local copies, waits for them, and re-layouts  27 us (10%)
  other arithmetic  19.3 us (7%)
  between operations  14.5 us (6%)
  starting transfers between devices  13.5 us (5%)
    ppermute x4, waiting for transfers between devices, shifted(): lax.ppermute(value, axis, [(source, source + steps) for source in range(f...  96 us
    reduce_scatter x1, waiting for transfers between devices, local(): lax.psum_scatter(returned, 'head', scatter_dimension=1, tiled=True)  52 us
    ppermute x4, starting transfers between devices, shifted(): lax.ppermute(value, axis, [(source, source + steps) for source in range(f...  13.5 us
    dot_general x3, matrix products, hop_grads(): jnp.einsum('tmgd,ugd->mgtu', g_heads, v_part, preferred_element_type=jnp....  12 us
    another operation x6, local copies, waits for them, and re-layouts, hop_grads(): return (new_query, jnp.stack([key_part, value_part]))  10.7 us
    dot_general x3, matrix products, add_values(): jnp.einsum('mgtu,ugd->tmgd', weights_b, v_part, preferred_element_type=jn...  7.93 us
    add x2, other arithmetic, local(): returned = partials[hop_index] + shifted(returned, 'ctx', -1)  7.66 us
    unnamed x52, local copies, waits for them, and re-layouts  7.44 us
  transfers between devices with their start and end apart: 5, of which 5 were waited for; matrix products, arithmetic and copies ran while one was open for 15% of the time, Pallas kernels for 0%

commit v1 on v0

v1 whole, which is shorter than its diff:
```python
import math

import jax
import jax.numpy as jnp
from jax import lax
from jax.experimental import pallas as pl
from jax.experimental.pallas import tpu as pltpu
from jax.sharding import PartitionSpec as P

HD = 128
KVH = 4
TOK = 512
HALF = 256
REACH = 1024
WIN = REACH + TOK
SPAN = REACH + HALF
STAGES = 2
MESH = pl.DeviceIdType.MESH
SCALE = 1.0 / math.sqrt(HD)
LOG2E = math.log2(math.e)
NT = (((1,), (1,)), ((), ()))
TN = (((0,), (0,)), ((), ()))


def mm(a, b):
    return jnp.dot(a, b, preferred_element_type=jnp.float32)


def kernel(
    ctx_size,
    q_ref, k_ref, v_ref, g_ref, len_ref,
    dq_ref, dk_ref, dv_ref,
    win, qo, pd, mine, dqs, begin,
    mate_out, mate_in, hop1, hop0, r2_out, r2_in, r1_out, r1_in, fin,
    load_sem, z1_s, z1_r, z2_s, z2_r, m1_s, m1_r, m2_s, m2_r, x_s, x_r,
    mt_s, mt_r, r2_s, r2_r, r1_s, r1_r, dq_s, dq_r, dq_l, f_s, f_r, f_l,
):
    ctx = lax.axis_index("ctx")
    head = lax.axis_index("head")
    core = lax.rem(head, 2)
    chip = head // 2
    other = 1 - core
    nxt = (lax.rem(ctx + 1, ctx_size), head)
    prv = (lax.rem(ctx + ctx_size - 1, ctx_size), head)
    mate = (ctx, chip * 2 + other)
    partner = (ctx, (1 - chip) * 2 + core)
    diagonal = (ctx, (1 - chip) * 2 + other)

    def cols(owner, s):
        return pl.ds(pl.multiple_of((owner * 2 + s) * HD, HD), HD)

    def remote(src, dst, send, recv, device):
        return pltpu.make_async_remote_copy(
            src_ref=src, dst_ref=dst, send_sem=send, recv_sem=recv,
            device_id=device, device_id_type=MESH,
        )

    own_rows = pl.ds(REACH, TOK)
    hop1_rows = pl.ds(TOK, TOK)
    hop2_rows = pl.ds(0, TOK)

    loads = []
    for s in range(STAGES):
        for kind, ref in ((0, k_ref), (1, v_ref)):
            loads.append(pltpu.make_async_copy(
                ref.at[:, cols(chip, s)], win.at[kind, s, own_rows], load_sem.at[kind, s]))
        for kind, ref in ((0, q_ref), (1, g_ref)):
            loads.append(pltpu.make_async_copy(
                ref.at[:, :, cols(chip, s)], qo.at[kind, s, :, 0], load_sem.at[2 + kind, s]))
    for load in loads:
        load.start()

    barrier = pltpu.get_barrier_semaphore()
    for device in (nxt, prv, mate, partner, diagonal):
        pl.semaphore_signal(barrier, 1, device_id=device, device_id_type=MESH)

    lengths = jnp.broadcast_to(len_ref[...], (64, 64)).astype(jnp.float32)
    upto = lax.broadcasted_iota(jnp.int32, (64, 64), 1) <= lax.broadcasted_iota(jnp.int32, (64, 64), 0)
    ends = jnp.sum(jnp.where(upto, lengths, 0.0), axis=1, keepdims=True).astype(jnp.int32)
    pos = lax.broadcasted_iota(jnp.int32, (64, TOK), 1) + ctx * TOK
    first = jnp.max(jnp.where(ends <= pos, ends, 0), axis=0, keepdims=True)
    begin[...] = jnp.broadcast_to(first - ctx * TOK + REACH, (8, TOK))

    for load in loads:
        load.wait()
    pl.semaphore_wait(barrier, 5)

    z1 = [remote(win.at[core, s, own_rows], win.at[core, s, hop1_rows], z1_s.at[s], z1_r.at[s], nxt)
          for s in range(STAGES)]
    z2 = [remote(win.at[core, s, hop1_rows], win.at[core, s, hop2_rows], z2_s.at[s], z2_r.at[s], nxt)
          for s in range(STAGES)]
    m1 = [remote(win.at[core, s, hop1_rows], win.at[core, s, hop1_rows], m1_s.at[s], m1_r.at[s], mate)
          for s in range(STAGES)]
    m1_in = [remote(win.at[other, s, hop1_rows], win.at[other, s, hop1_rows], m1_s.at[s], m1_r.at[s], mate)
             for s in range(STAGES)]
    m2 = [remote(win.at[core, s, hop2_rows], win.at[core, s, hop2_rows], m2_s.at[s], m2_r.at[s], mate)
          for s in range(STAGES)]
    m2_in = [remote(win.at[other, s, hop2_rows], win.at[other, s, hop2_rows], m2_s.at[s], m2_r.at[s], mate)
             for s in range(STAGES)]
    xq = [[remote(ref.at[:, :, cols(1 - chip, s)], qo.at[kind, s, :, 1], x_s.at[kind, s], x_r.at[kind, s], partner)
           for kind, ref in ((0, q_ref), (1, g_ref))] for s in range(STAGES)]
    mt = [remote(mate_out.at[s], mate_in.at[s], mt_s.at[s], mt_r.at[s], mate) for s in range(STAGES)]
    r2 = [remote(r2_out.at[s], r2_in.at[s], r2_s.at[s], r2_r.at[s], prv) for s in range(STAGES)]
    r1 = [remote(r1_out.at[s], r1_in.at[s], r1_s.at[s], r1_r.at[s], prv) for s in range(STAGES)]
    dq_far = [remote(dqs.at[s, 1], dq_ref.at[:, :, cols(chip, s)], dq_s.at[s], dq_r.at[s], partner)
              for s in range(STAGES)]
    dq_far_in = [remote(dqs.at[s, 1], dq_ref.at[:, :, cols(1 - chip, s)], dq_s.at[s], dq_r.at[s], partner)
                 for s in range(STAGES)]
    dq_near = [pltpu.make_async_copy(dqs.at[s, 0], dq_ref.at[:, :, cols(chip, s)], dq_l.at[s])
               for s in range(STAGES)]

    z1[0].start()
    for copy in xq[0]:
        copy.start()
    z1[1].start()
    for copy in xq[1]:
        copy.start()
    z1[0].wait_recv()
    z2[0].start()
    m1[0].start()

    causal = (lax.broadcasted_iota(jnp.int32, (HALF, HALF), 0)
              <= lax.broadcasted_iota(jnp.int32, (HALF, HALF), 1))
    place = lax.broadcasted_iota(jnp.int32, (SPAN, HALF), 0)

    def unit(s, c, j):
        rows = pl.ds(c * HALF, SPAN)
        k_win = win[0, s, rows]
        scores = lax.dot_general(k_win, qo[0, s, c, j], NT, preferred_element_type=jnp.float32)
        lowest = begin[0:1, c * HALF:(c + 1) * HALF] - c * HALF
        scores = jnp.where(place >= lowest, scores, -1e30)
        scores = jnp.concatenate(
            [scores[:REACH], jnp.where(causal, scores[REACH:], -1e30)], axis=0)
        top = jnp.max(scores, axis=0, keepdims=True)
        weights = jnp.exp2((scores - top) * (SCALE * LOG2E))
        inverse = 1.0 / jnp.sum(weights, axis=0, keepdims=True)
        grads = lax.dot_general(win[1, s, rows], qo[1, s, c, j], NT, preferred_element_type=jnp.float32)
        delta = jnp.sum(weights * grads, axis=0, keepdims=True) * inverse
        at = pl.ds(c * TOK + j * HALF, HALF)
        pd[1, rows, at] = (weights * inverse).astype(jnp.bfloat16)
        score_grads = (weights * (grads - delta) * (inverse * SCALE)).astype(jnp.bfloat16)
        pd[0, rows, at] = score_grads
        dqs[s, j, c] = lax.dot_general(
            score_grads, k_win, TN, preferred_element_type=jnp.float32).astype(jnp.bfloat16)

    pieces = ((0, HALF, 0, 1), (HALF, SPAN, 0, 2), (SPAN, WIN, 1, 2))

    def product(kind, s, piece):
        low, high, c0, c1 = piece
        right = qo[kind, s, c0:c1].reshape(((c1 - c0) * TOK, HD))
        return mm(pd[kind, low:high, c0 * TOK:c1 * TOK], right)

    def finish(s):
        r1[s].wait_recv()
        fin[s] = (hop0[s] + r1_in[s].astype(jnp.float32)).astype(jnp.bfloat16)
        for which, out in ((0, dk_ref), (1, dv_ref)):
            @pl.when(core == which)
            def _(out=out):
                for step, device in enumerate((partner, diagonal, mate)):
                    block = pl.ds(pl.multiple_of(device[1] * 128, 128), 128)
                    remote(fin.at[s, block], out.at[:, cols(chip, s)],
                           f_s.at[s, step], f_r.at[s, step], device).start()
                block = pl.ds(pl.multiple_of(head * 128, 128), 128)
                pltpu.make_async_copy(fin.at[s, block], out.at[:, cols(chip, s)], f_l.at[s]).start()

    def middle(s):
        r2[s].wait_recv()
        r1_out[s] = (hop1[s] + r2_in[s].astype(jnp.float32)).astype(jnp.bfloat16)
        r1[s].start()

    for s in range(STAGES):
        z2[s].wait_recv()
        m2[s].start()
        if s + 1 < STAGES:
            z1[s + 1].wait_recv()
            z2[s + 1].start()
            m1[s + 1].start()
        m1_in[s].wait_recv()
        m2_in[s].wait_recv()
        for c in range(2):
            unit(s, c, 0)
        for copy in xq[s]:
            copy.wait_recv()
        for c in range(2):
            unit(s, c, 1)
        dq_far[s].start()
        dq_near[s].start()
        for piece in pieces:
            mate_out[s, piece[0]:piece[1]] = product(other, s, piece).astype(jnp.bfloat16)
        mt[s].start()
        for piece in pieces:
            mine[piece[0]:piece[1]] = product(core, s, piece)
        mt[s].wait_recv()
        r2_out[s] = (mine[0:TOK] + mate_in[s, 0:TOK].astype(jnp.float32)).astype(jnp.bfloat16)
        r2[s].start()
        hop1[s] = mine[TOK:REACH] + mate_in[s, TOK:REACH].astype(jnp.float32)
        hop0[s] = mine[REACH:WIN] + mate_in[s, REACH:WIN].astype(jnp.float32)
        if s > 0:
            middle(s - 1)
    finish(0)
    middle(1)
    finish(1)

    for s in range(STAGES):
        for copy in (z1[s], z2[s], m1[s], m2[s], *xq[s], mt[s], r2[s], r1[s], dq_far[s]):
            copy.wait_send()
        dq_far_in[s].wait_recv()
        dq_near[s].wait()
        for which, out in ((0, dk_ref), (1, dv_ref)):
            @pl.when(core == which)
            def _(out=out, away=(dv_ref if which == 0 else dk_ref)):
                block = pl.ds(0, 128)
                for step, device in enumerate((partner, diagonal, mate)):
                    remote(fin.at[s, block], out.at[:, cols(chip, s)],
                           f_s.at[s, step], f_r.at[s, step], device).wait_send()
                remote(fin.at[s, block], out.at[:, cols(1 - chip, s)],
                       f_s.at[s, 0], f_r.at[s, 0], partner).wait_recv()
                remote(fin.at[s, block], away.at[:, cols(1 - chip, s)],
                       f_s.at[s, 1], f_r.at[s, 1], diagonal).wait_recv()
                remote(fin.at[s, block], away.at[:, cols(chip, s)],
                       f_s.at[s, 2], f_r.at[s, 2], mate).wait_recv()
                pltpu.make_async_copy(fin.at[s, block], out.at[:, cols(chip, s)], f_l.at[s]).wait()


def local(ctx_size, queries, keys, values, grad_out, doc_lengths):
    bf16, f32 = jnp.bfloat16, jnp.float32
    anywhere = pl.BlockSpec(memory_space=pl.ANY)
    pair = pltpu.SemaphoreType.DMA((STAGES,))
    block16 = pltpu.VMEM((STAGES, TOK, HD), bf16)
    block32 = pltpu.VMEM((STAGES, TOK, HD), f32)
    dq, dk, dv = pl.pallas_call(
        lambda *refs: kernel(ctx_size, *refs),
        out_shape=(
            jax.ShapeDtypeStruct((2, HALF, KVH * HD), bf16),
            jax.ShapeDtypeStruct((128, KVH * HD), bf16),
            jax.ShapeDtypeStruct((128, KVH * HD), bf16),
        ),
        in_specs=[anywhere] * 4 + [pl.BlockSpec(memory_space=pltpu.VMEM)],
        out_specs=(anywhere,) * 3,
        scratch_shapes=[
            pltpu.VMEM((2, STAGES, WIN, HD), bf16),
            pltpu.VMEM((2, STAGES, 2, 2, HALF, HD), bf16),
            pltpu.VMEM((2, WIN, 2 * TOK), bf16),
            pltpu.VMEM((WIN, HD), f32),
            pltpu.VMEM((STAGES, 2, 2, HALF, HD), bf16),
            pltpu.VMEM((8, TOK), jnp.int32),
            pltpu.VMEM((STAGES, WIN, HD), bf16),
            pltpu.VMEM((STAGES, WIN, HD), bf16),
            block32, block32,
            block16, block16, block16, block16, block16,
            pltpu.SemaphoreType.DMA((4, STAGES)),
            pair, pair, pair, pair, pair, pair, pair, pair,
            pltpu.SemaphoreType.DMA((2, STAGES)), pltpu.SemaphoreType.DMA((2, STAGES)),
            pair, pair, pair, pair, pair, pair, pair, pair, pair,
            pltpu.SemaphoreType.DMA((STAGES, 3)), pltpu.SemaphoreType.DMA((STAGES, 3)), pair,
        ],
        compiler_params=pltpu.CompilerParams(
            collective_id=0, has_side_effects=True, vmem_limit_bytes=56 * 2**20),
        cost_estimate=pl.CostEstimate(
            flops=10 * 4 * TOK * SPAN * HD, bytes_accessed=4 * 2**20, transcendentals=4 * TOK * SPAN),
        name="attention_backward",
    )(queries.reshape(2, HALF, KVH * HD), keys, values, grad_out.reshape(2, HALF, KVH * HD),
      doc_lengths.reshape(1, 64))
    return dq.reshape(TOK, 1, KVH * HD), dk, dv


def solution(mesh):
    placed = (P("ctx", "head", None), P("ctx", None), P("ctx", None), P("ctx", "head", None), P())
    ctx_size = mesh.shape["ctx"]
    return jax.shard_map(
        lambda *args: local(ctx_size, *args),
        mesh=mesh,
        in_specs=placed,
        out_specs=(P("ctx", "head", None), P(("ctx", "head"), None), P(("ctx", "head"), None)),
        check_vma=False,
    )
```

time: 261 us -> 63.1 us (0.24)
  waiting for transfers between devices: 148 us -> 0 us
  Pallas kernels: 0 us -> 58.8 us
  matrix products: 37.8 us -> 0 us
  local copies, waits for them, and re-layouts: 27 us -> 3.51 us
  other arithmetic: 19.3 us -> 0 us
  between operations: 14.5 us -> 0.65 us
  starting transfers between devices: 13.5 us -> 0 us
    ppermute x4 -> x0, waiting for transfers between devices: 96 us -> none  [shifted(): lax.ppermute(value, axis, [(source, source + steps) for source in range(f...]
    pallas_call x0 -> x1, Pallas kernels: none -> 58.8 us  [local(): pl.pallas_call(lambda *refs: kernel(ctx_size, *refs), out_shape=(jax.Shap...]
    reduce_scatter x1 -> x0, waiting for transfers between devices: 52 us -> none  [local(): lax.psum_scatter(returned, 'head', scatter_dimension=1, tiled=True)]
    dot_general x18 -> x0, matrix products: 37.8 us -> none  [the longest x3 12 us: hop_grads(): jnp.einsum('tmgd,ugd->mgtu', g_heads, v_part, preferred_element_type=jnp....]
    another operation x11 -> x0, local copies, waits for them, and re-layouts: 14.6 us -> none  [the longest x6 10.7 us: hop_grads(): return (new_query, jnp.stack([key_part, value_part]))]
    ppermute x4 -> x0, starting transfers between devices: 13.5 us -> none  [shifted(): lax.ppermute(value, axis, [(source, source + steps) for source in range(f...]
    add x5 -> x0, other arithmetic: 7.69 us -> none  [the longest x2 7.66 us: local(): returned = partials[hop_index] + shifted(returned, 'ctx', -1)]
    reduce_sum x4 -> x0, other arithmetic: 5.06 us -> none  [the longest x1 3.09 us: local(): row_total = jnp.sum(jnp.exp(first_scores - row_top), axis=-1, keepdims=True)]
  transfers between devices with their start and end apart: 5 -> 0, of which waited for: 5 -> 0; matrix products, arithmetic and copies ran while one was open for 15% -> 0% of each run, Pallas kernels for 0% -> 0%
where the time goes in v1:
time: 63.1 us; the launch traced here: 62.9 us
  Pallas kernels  58.8 us (93%)
  local copies, waits for them, and re-layouts  3.51 us (6%)
  between operations  0.65 us (1%)
    pallas_call x1, Pallas kernels, local(): pl.pallas_call(lambda *refs: kernel(ctx_size, *refs), out_shape=(jax.Shap...  58.8 us
    unnamed x7, local copies, waits for them, and re-layouts  3.51 us

profile of v1, /device:TPU:1, one launch (start us, length us, event | category | flops | bytes accessed | tf_op | source)
XLA Modules:
  0.0 62.9 jit_solution(4291247043194826219)
XLA Ops:
  0.6 58.8 %attention_backward.1 = (bf16[2,256,512]{2,1,0:T(8,128)(2,1)}, bf16[128,512]{1,0:T(8,128)(2,1)}, bf16[128,512]{1,0:T(8,128)(2,1)}) custom-call(bf16[2,256,512]{2,1,0:T(8,128)(2,1)} %bitcast.5, bf16[512,512]{1,0:T(8,128)(2,1)} %refs_1_.1, bf16[512,512]{1,0:T(8,128)(2,1)} %refs_2_.1, bf16[2,256,512]{2,1,0:T(8,128)(2,1)} %bitcast.6, s32[1,64]{1,0:T(1,128)} %bitcast.7), custom_call_target="tpu_custom_call" | custom-call | flops 3355443200 | bytes 4194304 | tf_op jit(solution)/shard_map/attention_backward/pallas_call | solution.py:231
  59.4 0.0 copy-start.1
  59.4 1.9 %copy.11 = bf16[512,1,512]{2,0,1:T(8,128)(2,1)} copy(bf16[512,1,512]{2,0,1:T(8,128)(2,1)} %bitcast.4) | data formatting | bytes 1048576
  61.3 0.0 copy-done.1
  61.3 0.0 copy-start
  61.3 0.7 %copy.12 = bf16[128,512]{1,0:T(8,128)(2,1)} copy(bf16[128,512]{1,0:T(8,128)(2,1)S(1)} %copy-done.1) | data formatting | bytes 262144
  62.0 0.3 copy-done
  62.3 0.7 %copy.13 = bf16[128,512]{1,0:T(8,128)(2,1)} copy(bf16[128,512]{1,0:T(8,128)(2,1)S(1)} %copy-done) | data formatting | bytes 262144
Async XLA Ops:
  59.4 1.9 %copy-start.1 = (bf16[128,512]{1,0:T(8,128)(2,1)S(1)}, bf16[128,512]{1,0:T(8,128)(2,1)}, u32[]{:S(2)}) copy-start(bf16[128,512]{1,0:T(8,128)(2,1)} %get-tuple-element.13) | copy-start | bytes 393220
  61.3 1.0 %copy-start = (bf16[128,512]{1,0:T(8,128)(2,1)S(1)}, bf16[128,512]{1,0:T(8,128)(2,1)}, u32[]{:S(2)}) copy-start(bf16[128,512]{1,0:T(8,128)(2,1)} %get-tuple-element.14) | copy-start | bytes 393220

commit v2 on v1

v2 whole, which is shorter than its diff:
```python
import math

import jax
import jax.numpy as jnp
from jax import lax
from jax.experimental import pallas as pl
from jax.experimental.pallas import tpu as pltpu
from jax.sharding import PartitionSpec as P

HD = 128
KVH = 4
TOK = 512
HALF = 256
REACH = 1024
WIN = REACH + TOK
SPAN = REACH + HALF
TILE = 64
STAGES = 2
MESH = pl.DeviceIdType.MESH
SCALE = 1.0 / math.sqrt(HD)
LOG2E = math.log2(math.e)
NT = (((1,), (1,)), ((), ()))
TN = (((0,), (0,)), ((), ()))


def mm(a, b):
    return jnp.dot(a, b, preferred_element_type=jnp.float32)


def kernel(
    ctx_size,
    q_ref, k_ref, v_ref, g_ref, len_ref,
    dq_ref, dk_ref, dv_ref,
    win, qo, pd, score, wgrad, mine, dqs, key_doc, query_doc,
    mate_out, mate_in, hop1, r2_out, r2_in, r1_out, r1_in, h0_out, h0_in,
    load_sem, z1_s, z1_r, z2_s, z2_r, m1_s, m1_r, m2_s, m2_r, x_s, x_r,
    mt_s, mt_r, r2_s, r2_r, r1_s, r1_r, dq_s, dq_r, dq_l, h0_s, h0_r,
):
    ctx = lax.axis_index("ctx")
    head = lax.axis_index("head")
    core = lax.rem(head, 2)
    chip = head // 2
    other = 1 - core
    nxt = (lax.rem(ctx + 1, ctx_size), head)
    prv = (lax.rem(ctx + ctx_size - 1, ctx_size), head)
    mate = (ctx, chip * 2 + other)
    partner = (ctx, (1 - chip) * 2 + core)
    diagonal = (ctx, (1 - chip) * 2 + other)
    stages, halves = range(STAGES), range(2)

    def cols(owner, s):
        return pl.ds(pl.multiple_of((owner * 2 + s) * HD, HD), HD)

    def remote(src, dst, send, recv, device):
        return pltpu.make_async_remote_copy(
            src_ref=src, dst_ref=dst, send_sem=send, recv_sem=recv,
            device_id=device, device_id_type=MESH,
        )

    own_rows = pl.ds(REACH, TOK)
    hop1_rows = pl.ds(TOK, TOK)
    hop2_rows = pl.ds(0, TOK)

    loads = []
    for s in stages:
        for kind, ref in ((0, k_ref), (1, v_ref)):
            loads.append(pltpu.make_async_copy(
                ref.at[:, cols(chip, s)], win.at[kind, s, own_rows], load_sem.at[kind, s]))
        for kind, ref in ((0, q_ref), (1, g_ref)):
            loads.append(pltpu.make_async_copy(
                ref.at[:, :, cols(chip, s)], qo.at[kind, s, :, 0], load_sem.at[2 + kind, s]))
    for load in loads:
        load.start()

    barrier = pltpu.get_barrier_semaphore()
    for device in (mate, partner, diagonal, *[(nxt[0], h) for h in range(4)], *[(prv[0], h) for h in range(4)]):
        pl.semaphore_signal(barrier, 1, device_id=device, device_id_type=MESH)

    for load in loads:
        load.wait()
    pl.semaphore_wait(barrier, 11)

    z1 = [remote(win.at[core, s, own_rows], win.at[core, s, hop1_rows], z1_s.at[s], z1_r.at[s], nxt) for s in stages]
    z2 = [remote(win.at[core, s, hop1_rows], win.at[core, s, hop2_rows], z2_s.at[s], z2_r.at[s], nxt) for s in stages]
    m1 = [remote(win.at[core, s, hop1_rows], win.at[core, s, hop1_rows], m1_s.at[s], m1_r.at[s], mate)
          for s in stages]
    m1_in = [remote(win.at[other, s, hop1_rows], win.at[other, s, hop1_rows], m1_s.at[s], m1_r.at[s], mate)
             for s in stages]
    m2 = [remote(win.at[core, s, hop2_rows], win.at[core, s, hop2_rows], m2_s.at[s], m2_r.at[s], mate)
          for s in stages]
    m2_in = [remote(win.at[other, s, hop2_rows], win.at[other, s, hop2_rows], m2_s.at[s], m2_r.at[s], mate)
             for s in stages]
    xq = [[remote(ref.at[:, :, cols(1 - chip, s)], qo.at[kind, s, :, 1], x_s.at[kind, s], x_r.at[kind, s], partner)
           for kind, ref in ((0, q_ref), (1, g_ref))] for s in stages]
    mate_rows = (hop2_rows, pl.ds(TOK, 2 * TOK))
    mt = [[remote(mate_out.at[s, mate_rows[h]], mate_in.at[s, mate_rows[h]], mt_s.at[s, h], mt_r.at[s, h], mate)
           for h in halves] for s in stages]
    quarters = [pl.ds(q * 128, 128) for q in range(4)]
    r2 = [[remote(r2_out.at[s, rows], r2_in.at[s, rows], r2_s.at[s, q], r2_r.at[s, q], prv)
           for q, rows in enumerate(quarters)] for s in stages]
    r1 = [[remote(r1_out.at[s, rows], r1_in.at[s, head], r1_s.at[s, q], r1_r.at[s, head], (prv[0], q))
           for q, rows in enumerate(quarters)] for s in stages]
    r1_from = [[remote(r1_out.at[s, quarters[0]], r1_in.at[s, h], r1_s.at[s, 0], r1_r.at[s, h], prv)
                for h in range(4)] for s in stages]
    h0 = [[remote(h0_out.at[s, rows], h0_in.at[s, head], h0_s.at[s, q], h0_r.at[s, head], (ctx, q))
           for q, rows in enumerate(quarters)] for s in stages]
    h0_from = [[remote(h0_out.at[s, quarters[0]], h0_in.at[s, h], h0_s.at[s, 0], h0_r.at[s, h], mate)
                for h in range(4)] for s in stages]
    dq_far = [remote(dqs.at[s, 1], dq_ref.at[:, :, cols(chip, s)], dq_s.at[s], dq_r.at[s], partner)
              for s in stages]
    dq_far_in = [remote(dqs.at[s, 1], dq_ref.at[:, :, cols(1 - chip, s)], dq_s.at[s], dq_r.at[s], partner)
                 for s in stages]
    dq_near = [pltpu.make_async_copy(dqs.at[s, 0], dq_ref.at[:, :, cols(chip, s)], dq_l.at[s])
               for s in stages]

    for copy in (*z1, *xq[0], *xq[1]):
        copy.start()

    lengths = len_ref[...]
    upto = jnp.where(
        lax.broadcasted_iota(jnp.int32, (64, HD), 0) <= lax.broadcasted_iota(jnp.int32, (64, HD), 1), 1.0, 0.0
    ).astype(jnp.bfloat16)

    def ends_of(part):
        rows = jnp.broadcast_to(part, (16, 64)).astype(jnp.float32).astype(jnp.bfloat16)
        return mm(rows, upto)[0:1]

    ends = (ends_of(lengths >> 5) * 32.0 + ends_of(lengths & 31)).astype(jnp.int32)
    wide = (16, 64)
    before = jnp.where(
        lax.broadcasted_iota(jnp.int32, (64, HD), 0) < lax.broadcasted_iota(jnp.int32, (64, HD), 1), 1.0, 0.0
    ).astype(jnp.bfloat16)

    def starts_of(part):
        rows = jnp.broadcast_to(part, wide).astype(jnp.float32).astype(jnp.bfloat16)
        return mm(rows, before)[0:1]

    starts = (starts_of(lengths >> 5) * 32.0 + starts_of(lengths & 31)).astype(jnp.int32)
    lane = lax.broadcasted_iota(jnp.int32, (1, HD), 1)
    starts = jnp.where(lane == 64, -WIN, starts)
    ends = jnp.where(lane == 64, 0, ends)

    def inside(count, base):
        pos = lax.broadcasted_iota(jnp.int32, (count, HD), 0) + base
        return (starts <= pos) & (pos < ends)

    for t in range(0, WIN, HALF):
        key_doc[t:t + HALF] = jnp.where(inside(HALF, ctx * TOK - REACH + t), 1.0, 0.0).astype(jnp.bfloat16)
    for t in range(0, TOK, HALF):
        query_doc[t:t + HALF] = jnp.where(inside(HALF, ctx * TOK + t), 0.0, -1e30).astype(jnp.bfloat16)

    causal = (lax.broadcasted_iota(jnp.int32, (HALF, HALF), 0)
              <= lax.broadcasted_iota(jnp.int32, (HALF, HALF), 1))

    def fold(x):
        return jnp.sum(x.reshape(x.shape[0] // 8, 8, x.shape[1]), axis=0)

    tiles = tuple(range(0, SPAN, TILE))

    def unit(s, c, j):
        low = c * HALF
        rows = pl.ds(low, SPAN)
        keyed = jnp.concatenate([win[0, s, rows], key_doc[rows]], axis=1)
        asked = jnp.concatenate([qo[0, s, c, j], query_doc[low:low + HALF]], axis=1)
        score[...] = lax.dot_general(keyed, asked, NT, preferred_element_type=jnp.float32)
        wgrad[...] = lax.dot_general(
            win[1, s, rows], qo[1, s, c, j], NT, preferred_element_type=jnp.float32)
        diagonal_rows = jnp.where(causal, score[REACH:SPAN], -1e30)
        score[REACH:SPAN] = diagonal_rows
        peak = None
        for t in tiles:
            x = score[t:t + TILE]
            x = jnp.max(x.reshape(TILE // 8, 8, HALF), axis=0)
            peak = x if peak is None else jnp.maximum(peak, x)
        top = jnp.max(peak, axis=0, keepdims=True)
        total = jnp.zeros((8, HALF), jnp.float32)
        dots = jnp.zeros((8, HALF), jnp.float32)
        for t in tiles:
            e = jnp.exp2((score[t:t + TILE] - top) * (SCALE * LOG2E))
            score[t:t + TILE] = e
            total += fold(e)
            dots += fold(e * wgrad[t:t + TILE])
        inverse = 1.0 / jnp.sum(total, axis=0, keepdims=True)
        delta = jnp.sum(dots, axis=0, keepdims=True) * inverse
        at = pl.ds(c * TOK + j * HALF, HALF)
        for t in tiles:
            weights = score[t:t + TILE] * inverse
            pd[s, 1, low + t:low + t + TILE, at] = weights.astype(jnp.bfloat16)
            pd[s, 0, low + t:low + t + TILE, at] = (weights * (wgrad[t:t + TILE] - delta)).astype(jnp.bfloat16)

    def query_grads(s):
        for c in halves:
            rows = pl.ds(c * HALF, SPAN)
            found = lax.dot_general(
                pd[s, 0, rows, c * TOK:(c + 1) * TOK], win[0, s, rows], TN, preferred_element_type=jnp.float32)
            dqs[s, :, c] = (found * SCALE).astype(jnp.bfloat16).reshape(2, HALF, HD)
        dq_far[s].start()
        dq_near[s].start()

    pieces = (((0, HALF, 0, 1), (HALF, TOK, 0, 2)), ((TOK, SPAN, 0, 2), (SPAN, WIN, 1, 2)))

    def product(kind, s, piece):
        low, high, c0, c1 = piece
        right = qo[kind, s, c0:c1].reshape(((c1 - c0) * TOK, HD))
        return mm(pd[s, kind, low:high, c0 * TOK:c1 * TOK], right) * jnp.where(kind == 0, SCALE, 1.0)

    def theirs(s, h):
        for piece in pieces[h]:
            mate_out[s, piece[0]:piece[1]] = product(other, s, piece).astype(jnp.bfloat16)
        mt[s][h].start()

    def ours(s, h):
        for piece in pieces[h]:
            mine[piece[0]:piece[1]] = product(core, s, piece)

    def outer(s):
        theirs(s, 0)
        ours(s, 0)
        theirs(s, 1)
        mt[s][0].wait_recv()
        for q in range(4):
            at = slice(q * 128, (q + 1) * 128)
            r2_out[s, at] = (mine[at] + mate_in[s, at].astype(jnp.float32)).astype(jnp.bfloat16)
            r2[s][q].start()
        ours(s, 1)
        mt[s][1].wait_recv()
        hop1[s] = mine[TOK:REACH] + mate_in[s, TOK:REACH].astype(jnp.float32)
        h0_out[s] = (mine[REACH:WIN] + mate_in[s, REACH:WIN].astype(jnp.float32)).astype(jnp.bfloat16)
        for q in range(4):
            @pl.when(head != q)
            def _(q=q):
                h0[s][q].start()

            @pl.when(head == q)
            def _(q=q):
                pltpu.make_async_copy(h0_out.at[s, quarters[q]], h0_in.at[s, q], h0_r.at[s, q]).start()

    def middle(s):
        for q in range(4):
            at = slice(q * 128, (q + 1) * 128)
            r2[s][q].wait_recv()
            r1_out[s, at] = (hop1[s, at] + r2_in[s, at].astype(jnp.float32)).astype(jnp.bfloat16)
            r1[s][q].start()

    def finish(s):
        for h in range(4):
            h0_from[s][h].wait_recv()
            r1_from[s][h].wait_recv()
            out = (dk_ref, dv_ref)[h % 2]
            g = (h // 2) * 2 + s
            out[:, g * HD:(g + 1) * HD] = (
                h0_in[s, h].astype(jnp.float32) + r1_in[s, h].astype(jnp.float32)).astype(jnp.bfloat16)

    def forward(s):
        z1[s].wait_recv()
        z2[s].start()
        m1[s].start()

    def arrive(s):
        z2[s].wait_recv()
        m2[s].start()

    forward(0)
    forward(1)
    arrive(0)
    m1_in[0].wait_recv()
    m2_in[0].wait_recv()
    unit(0, 0, 0)
    unit(0, 1, 0)
    for copy in xq[0]:
        copy.wait_recv()
    unit(0, 0, 1)
    arrive(1)
    unit(0, 1, 1)
    outer(0)
    m1_in[1].wait_recv()
    m2_in[1].wait_recv()
    unit(1, 0, 0)
    unit(1, 1, 0)
    middle(0)
    for copy in xq[1]:
        copy.wait_recv()
    unit(1, 0, 1)
    unit(1, 1, 1)
    outer(1)
    query_grads(1)
    query_grads(0)
    middle(1)
    finish(0)
    finish(1)

    for s in stages:
        for copy in (z1[s], z2[s], m1[s], m2[s], *xq[s], *mt[s], *r2[s], *r1[s], dq_far[s]):
            copy.wait_send()
        for q in range(4):
            @pl.when(head != q)
            def _(q=q):
                h0[s][q].wait_send()
        dq_far_in[s].wait_recv()
        dq_near[s].wait()


def local(ctx_size, queries, keys, values, grad_out, doc_lengths):
    bf16, f32 = jnp.bfloat16, jnp.float32
    anywhere = pl.BlockSpec(memory_space=pl.ANY)
    pair = pltpu.SemaphoreType.DMA((STAGES,))
    quad = pltpu.SemaphoreType.DMA((STAGES, 2))
    eight = pltpu.SemaphoreType.DMA((STAGES, 4))
    block16 = pltpu.VMEM((STAGES, TOK, HD), bf16)
    heads16 = pltpu.VMEM((STAGES, 4, 128, HD), bf16)
    dq, dk, dv = pl.pallas_call(
        lambda *refs: kernel(ctx_size, *refs),
        out_shape=(
            pltpu.VMEM((2, HALF, KVH * HD), bf16),
            pltpu.VMEM((128, KVH * HD), bf16),
            pltpu.VMEM((128, KVH * HD), bf16),
        ),
        in_specs=[anywhere] * 4 + [pl.BlockSpec(memory_space=pltpu.VMEM)],
        out_specs=(pl.BlockSpec(memory_space=pltpu.VMEM), pl.BlockSpec(memory_space=pltpu.VMEM), pl.BlockSpec(memory_space=pltpu.VMEM)),
        scratch_shapes=[
            pltpu.VMEM((2, STAGES, WIN, HD), bf16),
            pltpu.VMEM((2, STAGES, 2, 2, HALF, HD), bf16),
            pltpu.VMEM((STAGES, 2, WIN, 2 * TOK), bf16),
            pltpu.VMEM((SPAN, HALF), f32),
            pltpu.VMEM((SPAN, HALF), f32),
            pltpu.VMEM((WIN, HD), f32),
            pltpu.VMEM((STAGES, 2, 2, HALF, HD), bf16),
            pltpu.VMEM((WIN, HD), bf16),
            pltpu.VMEM((TOK, HD), bf16),
            pltpu.VMEM((STAGES, WIN, HD), bf16),
            pltpu.VMEM((STAGES, WIN, HD), bf16),
            pltpu.VMEM((STAGES, TOK, HD), f32),
            block16, block16, block16, heads16, block16, heads16,
            pltpu.SemaphoreType.DMA((4, STAGES)),
            pair, pair, pair, pair, pair, pair, pair, pair,
            quad, quad,
            quad, quad, eight, eight, eight, eight, pair, pair, pair,
            eight, eight,
        ],
        compiler_params=pltpu.CompilerParams(
            collective_id=0, has_side_effects=True, vmem_limit_bytes=56 * 2**20),
        cost_estimate=pl.CostEstimate(
            flops=10 * 4 * TOK * SPAN * HD, bytes_accessed=4 * 2**20, transcendentals=4 * TOK * SPAN),
        name="attention_backward",
    )(queries.reshape(2, HALF, KVH * HD), keys, values, grad_out.reshape(2, HALF, KVH * HD),
      doc_lengths.reshape(1, 64))
    return dq.reshape(TOK, 1, KVH * HD), dk, dv


def solution(mesh):
    placed = (P("ctx", "head", None), P("ctx", None), P("ctx", None), P("ctx", "head", None), P())
    ctx_size = mesh.shape["ctx"]
    return jax.shard_map(
        lambda *args: local(ctx_size, *args),
        mesh=mesh,
        in_specs=placed,
        out_specs=(P("ctx", "head", None), P(("ctx", "head"), None), P(("ctx", "head"), None)),
        check_vma=False,
    )
```

time: 63.1 us -> 55.3 us (0.88)
  Pallas kernels: 58.8 us -> 52.5 us
  local copies, waits for them, and re-layouts: 3.51 us -> 2.11 us
    pallas_call x1, Pallas kernels: 58.8 us -> 52.5 us  [local(): pl.pallas_call(lambda *refs: kernel(ctx_size, *refs), out_shape=(pltpu.VM...]
    unnamed x7 -> x3, local copies, waits for them, and re-layouts: 3.51 us -> 2.11 us
where the time goes in v2:
time: 55.3 us; the launch traced here: 55.2 us
  Pallas kernels  52.5 us (95%)
  local copies, waits for them, and re-layouts  2.11 us (4%)
  between operations  0.64 us (1%)
    pallas_call x1, Pallas kernels, local(): pl.pallas_call(lambda *refs: kernel(ctx_size, *refs), out_shape=(pltpu.VM...  52.5 us
    unnamed x3, local copies, waits for them, and re-layouts  2.11 us

profile of v2, /device:TPU:1, one launch (start us, length us, event | category | flops | bytes accessed | tf_op | source)
XLA Modules:
  0.0 55.2 jit_solution(6808365797901077342)
XLA Ops:
  0.6 52.5 %attention_backward.1 = (bf16[2,256,512]{2,1,0:T(8,128)(2,1)S(1)}, bf16[128,512]{1,0:T(8,128)(2,1)S(1)}, bf16[128,512]{1,0:T(8,128)(2,1)S(1)}) custom-call(bf16[2,256,512]{2,1,0:T(8,128)(2,1)} %bitcast.5, bf16[512,512]{1,0:T(8,128)(2,1)} %refs_1_.1, bf16[512,512]{1,0:T(8,128)(2,1)} %refs_2_.1, bf16[2,256,512]{2,1,0:T(8,128)(2,1)} %bitcast.6, s32[1,64]{1,0:T(1,128)} %bitcast.7), custom_call_target="tpu_custom_call" | custom-call | flops 3355443200 | bytes 4194304 | tf_op jit(solution)/shard_map/attention_backward/pallas_call | solution.py:311
  53.1 0.8 %copy.11 = bf16[512,1,512]{2,0,1:T(8,128)(2,1)} copy(bf16[512,1,512]{2,0,1:T(8,128)(2,1)S(1)} %bitcast.4) | data formatting | bytes 1048576
  53.9 0.7 %copy.12 = bf16[128,512]{1,0:T(8,128)(2,1)} copy(bf16[128,512]{1,0:T(8,128)(2,1)S(1)} %get-tuple-element.10) | data formatting | bytes 262144
  54.6 0.7 %copy.13 = bf16[128,512]{1,0:T(8,128)(2,1)} copy(bf16[128,512]{1,0:T(8,128)(2,1)S(1)} %get-tuple-element.11) | data formatting | bytes 262144

commit v3 on v2

--- a/solution.py
+++ b/solution.py
@@ -16,6 +16,7 @@
 SPAN = REACH + HALF
 TILE = 64
 STAGES = 2
+ROW = 8
 MESH = pl.DeviceIdType.MESH
 SCALE = 1.0 / math.sqrt(HD)
 LOG2E = math.log2(math.e)
@@ -31,10 +32,10 @@
     ctx_size,
     q_ref, k_ref, v_ref, g_ref, len_ref,
     dq_ref, dk_ref, dv_ref,
-    win, qo, pd, score, wgrad, mine, dqs, key_doc, query_doc,
-    mate_out, mate_in, hop1, r2_out, r2_in, r1_out, r1_in, h0_out, h0_in,
+    win, qo, pd, score_a, score_b, wgrad_a, wgrad_b, mine, dqs, key_doc, query_doc,
+    mate_out, mate_in, hop1, r2_out, r2_in, r1_out, r1_in, h0_out, h0_in, relay,
     load_sem, z1_s, z1_r, z2_s, z2_r, m1_s, m1_r, m2_s, m2_r, x_s, x_r,
-    mt_s, mt_r, r2_s, r2_r, r1_s, r1_r, dq_s, dq_r, dq_l, h0_s, h0_r,
+    mt_s, mt_r, r2_s, r2_r, r1_s, r1_r, dq_s, dq_r, dq_l, h0_s, h0_r, relay_s, relay_r,
 ):
     ctx = lax.axis_index("ctx")
     head = lax.axis_index("head")
@@ -47,6 +48,13 @@
     partner = (ctx, (1 - chip) * 2 + core)
     diagonal = (ctx, (1 - chip) * 2 + other)
     stages, halves = range(STAGES), range(2)
+    place = lax.rem(ctx, ROW)
+    at_start, at_end = place == 0, place == ROW - 1
+
+    def near(steps):
+        return (lax.rem(ctx + ctx_size + steps, ctx_size), head)
+
+    relay_to, relay_from, relay_down, relay_up = near(ROW), near(-ROW), near(1 - ROW), near(ROW - 1)
 
     def cols(owner, s):
         return pl.ds(pl.multiple_of((owner * 2 + s) * HD, HD), HD)
@@ -76,12 +84,25 @@
     for device in (mate, partner, diagonal, *[(nxt[0], h) for h in range(4)], *[(prv[0], h) for h in range(4)]):
         pl.semaphore_signal(barrier, 1, device_id=device, device_id_type=MESH)
 
+    @pl.when(at_end)
+    def _():
+        for device in (relay_to, relay_from, relay_down):
+            pl.semaphore_signal(barrier, 1, device_id=device, device_id_type=MESH)
+
+    @pl.when(at_start)
+    def _():
+        pl.semaphore_signal(barrier, 1, device_id=relay_up, device_id_type=MESH)
+
     for load in loads:
         load.wait()
-    pl.semaphore_wait(barrier, 11)
+    pl.semaphore_wait(barrier, 11 + 3 * (place // (ROW - 1)) + (ROW - 1 - place) // (ROW - 1))
 
     z1 = [remote(win.at[core, s, own_rows], win.at[core, s, hop1_rows], z1_s.at[s], z1_r.at[s], nxt) for s in stages]
     z2 = [remote(win.at[core, s, hop1_rows], win.at[core, s, hop2_rows], z2_s.at[s], z2_r.at[s], nxt) for s in stages]
+    z1_relayed = remote(win.at[core, 1, own_rows], relay.at[0], z1_s.at[1], relay_r.at[0], relay_to)
+    z2_relayed = remote(win.at[core, 1, hop1_rows], relay.at[1], z2_s.at[1], relay_r.at[1], relay_to)
+    passed = [remote(relay.at[k], win.at[core, 1, rows], relay_s.at[k], sem.at[1], relay_down)
+              for k, (rows, sem) in enumerate(((hop1_rows, z1_r), (hop2_rows, z2_r)))]
     m1 = [remote(win.at[core, s, hop1_rows], win.at[core, s, hop1_rows], m1_s.at[s], m1_r.at[s], mate)
           for s in stages]
     m1_in = [remote(win.at[other, s, hop1_rows], win.at[other, s, hop1_rows], m1_s.at[s], m1_r.at[s], mate)
@@ -113,7 +134,19 @@
     dq_near = [pltpu.make_async_copy(dqs.at[s, 0], dq_ref.at[:, :, cols(chip, s)], dq_l.at[s])
                for s in stages]
 
-    for copy in (*z1, *xq[0], *xq[1]):
+    z1[0].start()
+
+    def either(direct, relayed):
+        @pl.when(at_end)
+        def _():
+            relayed.start()
+
+        @pl.when(jnp.logical_not(at_end))
+        def _():
+            direct.start()
+
+    either(z1[1], z1_relayed)
+    for copy in (*xq[0], *xq[1]):
         copy.start()
 
     lengths = len_ref[...]
@@ -155,18 +188,23 @@
     def fold(x):
         return jnp.sum(x.reshape(x.shape[0] // 8, 8, x.shape[1]), axis=0)
 
+    scores, wgrads = (score_a, score_b), (wgrad_a, wgrad_b)
     tiles = tuple(range(0, SPAN, TILE))
 
-    def unit(s, c, j):
+    def open_unit(s, c, j, slot):
         low = c * HALF
         rows = pl.ds(low, SPAN)
+        score, wgrad = scores[slot], wgrads[slot]
         keyed = jnp.concatenate([win[0, s, rows], key_doc[rows]], axis=1)
         asked = jnp.concatenate([qo[0, s, c, j], query_doc[low:low + HALF]], axis=1)
         score[...] = lax.dot_general(keyed, asked, NT, preferred_element_type=jnp.float32)
         wgrad[...] = lax.dot_general(
             win[1, s, rows], qo[1, s, c, j], NT, preferred_element_type=jnp.float32)
-        diagonal_rows = jnp.where(causal, score[REACH:SPAN], -1e30)
-        score[REACH:SPAN] = diagonal_rows
+
+    def close_unit(s, c, j, slot):
+        low = c * HALF
+        score, wgrad = scores[slot], wgrads[slot]
+        score[REACH:SPAN] = jnp.where(causal, score[REACH:SPAN], -1e30)
         peak = None
         for t in tiles:
             x = score[t:t + TILE]
@@ -253,41 +291,74 @@
 
     def forward(s):
         z1[s].wait_recv()
-        z2[s].start()
+        if s == 1:
+            either(z2[1], z2_relayed)
+        else:
+            z2[s].start()
         m1[s].start()
+
+    def pass_on(k):
+        @pl.when(at_end)
+        def _():
+            (z1_relayed, z2_relayed)[k].wait_recv()
+            passed[k].start()
 
     def arrive(s):
         z2[s].wait_recv()
         m2[s].start()
 
     forward(0)
-    forward(1)
+
+    @pl.when(jnp.logical_not(at_start))
+    def _():
+        forward(1)
+
+    pass_on(0)
     arrive(0)
     m1_in[0].wait_recv()
     m2_in[0].wait_recv()
-    unit(0, 0, 0)
-    unit(0, 1, 0)
+    open_unit(0, 0, 0, 0)
+    open_unit(0, 1, 0, 1)
+    close_unit(0, 0, 0, 0)
+
+    @pl.when(at_start)
+    def _():
+        forward(1)
+
     for copy in xq[0]:
         copy.wait_recv()
-    unit(0, 0, 1)
+    open_unit(0, 0, 1, 0)
+    close_unit(0, 1, 0, 1)
+    pass_on(1)
+    open_unit(0, 1, 1, 1)
+    close_unit(0, 0, 1, 0)
+    close_unit(0, 1, 1, 1)
+    outer(0)
     arrive(1)
-    unit(0, 1, 1)
-    outer(0)
+    query_grads(0)
     m1_in[1].wait_recv()
     m2_in[1].wait_recv()
-    unit(1, 0, 0)
-    unit(1, 1, 0)
-    middle(0)
+    open_unit(1, 0, 0, 0)
+    open_unit(1, 1, 0, 1)
+    close_unit(1, 0, 0, 0)
     for copy in xq[1]:
         copy.wait_recv()
-    unit(1, 0, 1)
-    unit(1, 1, 1)
+    open_unit(1, 0, 1, 0)
+    close_unit(1, 1, 0, 1)
+    middle(0)
+    open_unit(1, 1, 1, 1)
+    close_unit(1, 0, 1, 0)
+    close_unit(1, 1, 1, 1)
     outer(1)
     query_grads(1)
-    query_grads(0)
     middle(1)
     finish(0)
     finish(1)
+
+    @pl.when(at_end)
+    def _():
+        for copy in passed:
+            copy.wait_send()
 
     for s in stages:
         for copy in (z1[s], z2[s], m1[s], m2[s], *xq[s], *mt[s], *r2[s], *r1[s], dq_far[s]):
@@ -307,6 +378,7 @@
     quad = pltpu.SemaphoreType.DMA((STAGES, 2))
     eight = pltpu.SemaphoreType.DMA((STAGES, 4))
     block16 = pltpu.VMEM((STAGES, TOK, HD), bf16)
+    unit32 = pltpu.VMEM((SPAN, HALF), f32)
     heads16 = pltpu.VMEM((STAGES, 4, 128, HD), bf16)
     dq, dk, dv = pl.pallas_call(
         lambda *refs: kernel(ctx_size, *refs),
@@ -321,8 +393,7 @@
             pltpu.VMEM((2, STAGES, WIN, HD), bf16),
             pltpu.VMEM((2, STAGES, 2, 2, HALF, HD), bf16),
             pltpu.VMEM((STAGES, 2, WIN, 2 * TOK), bf16),
-            pltpu.VMEM((SPAN, HALF), f32),
-            pltpu.VMEM((SPAN, HALF), f32),
+            unit32, unit32, unit32, unit32,
             pltpu.VMEM((WIN, HD), f32),
             pltpu.VMEM((STAGES, 2, 2, HALF, HD), bf16),
             pltpu.VMEM((WIN, HD), bf16),
@@ -331,11 +402,13 @@
             pltpu.VMEM((STAGES, WIN, HD), bf16),
             pltpu.VMEM((STAGES, TOK, HD), f32),
             block16, block16, block16, heads16, block16, heads16,
+            block16,
             pltpu.SemaphoreType.DMA((4, STAGES)),
             pair, pair, pair, pair, pair, pair, pair, pair,
             quad, quad,
             quad, quad, eight, eight, eight, eight, pair, pair, pair,
             eight, eight,
+            pair, pair,
         ],
         compiler_params=pltpu.CompilerParams(
             collective_id=0, has_side_effects=True, vmem_limit_bytes=56 * 2**20),

time: 55.3 us -> 53.8 us (0.973)
  Pallas kernels: 52.5 us -> 50.9 us
    pallas_call x1, Pallas kernels: 52.5 us -> 50.9 us  [local(): pl.pallas_call(lambda *refs: kernel(ctx_size, *refs), out_shape=(pltpu.VM...]
where the time goes in v3:
time: 53.8 us; the launch traced here: 53.7 us
  Pallas kernels  50.9 us (95%)
  local copies, waits for them, and re-layouts  2.11 us (4%)
  between operations  0.64 us (1%)
    pallas_call x1, Pallas kernels, local(): pl.pallas_call(lambda *refs: kernel(ctx_size, *refs), out_shape=(pltpu.VM...  50.9 us
    unnamed x3, local copies, waits for them, and re-layouts  2.11 us

profile of v3, /device:TPU:1, one launch (start us, length us, event | category | flops | bytes accessed | tf_op | source)
XLA Modules:
  0.0 53.7 jit_solution(11845005999354685466)
XLA Ops:
  0.6 50.9 %attention_backward.1 = (bf16[2,256,512]{2,1,0:T(8,128)(2,1)S(1)}, bf16[128,512]{1,0:T(8,128)(2,1)S(1)}, bf16[128,512]{1,0:T(8,128)(2,1)S(1)}) custom-call(bf16[2,256,512]{2,1,0:T(8,128)(2,1)} %bitcast.5, bf16[512,512]{1,0:T(8,128)(2,1)} %refs_1_.1, bf16[512,512]{1,0:T(8,128)(2,1)} %refs_2_.1, bf16[2,256,512]{2,1,0:T(8,128)(2,1)} %bitcast.6, s32[1,64]{1,0:T(1,128)} %bitcast.7), custom_call_target="tpu_custom_call" | custom-call | flops 3355443200 | bytes 4194304 | tf_op jit(solution)/shard_map/attention_backward/pallas_call | solution.py:383
  51.6 0.8 %copy.11 = bf16[512,1,512]{2,0,1:T(8,128)(2,1)} copy(bf16[512,1,512]{2,0,1:T(8,128)(2,1)S(1)} %bitcast.4) | data formatting | bytes 1048576
  52.4 0.7 %copy.12 = bf16[128,512]{1,0:T(8,128)(2,1)} copy(bf16[128,512]{1,0:T(8,128)(2,1)S(1)} %get-tuple-element.10) | data formatting | bytes 262144
  53.0 0.7 %copy.13 = bf16[128,512]{1,0:T(8,128)(2,1)} copy(bf16[128,512]{1,0:T(8,128)(2,1)S(1)} %get-tuple-element.11) | data formatting | bytes 262144

commit v4 on v3

--- a/solution.py
+++ b/solution.py
@@ -32,7 +32,7 @@
     ctx_size,
     q_ref, k_ref, v_ref, g_ref, len_ref,
     dq_ref, dk_ref, dv_ref,
-    win, qo, pd, score_a, score_b, wgrad_a, wgrad_b, mine, dqs, key_doc, query_doc,
+    win, qo, pd, scores, wgrads, stats, mine, dqs, key_doc, query_doc,
     mate_out, mate_in, hop1, r2_out, r2_in, r1_out, r1_in, h0_out, h0_in, relay,
     load_sem, z1_s, z1_r, z2_s, z2_r, m1_s, m1_r, m2_s, m2_r, x_s, x_r,
     mt_s, mt_r, r2_s, r2_r, r1_s, r1_r, dq_s, dq_r, dq_l, h0_s, h0_r, relay_s, relay_r,
@@ -188,43 +188,55 @@
     def fold(x):
         return jnp.sum(x.reshape(x.shape[0] // 8, 8, x.shape[1]), axis=0)
 
-    scores, wgrads = (score_a, score_b), (wgrad_a, wgrad_b)
-    tiles = tuple(range(0, SPAN, TILE))
-
-    def open_unit(s, c, j, slot):
-        low = c * HALF
-        rows = pl.ds(low, SPAN)
-        score, wgrad = scores[slot], wgrads[slot]
+    slots = {(0, 0): 0, (0, 1): 2, (1, 0): 4, (1, 1): 0}
+
+    def part(s, c, j, low, high):
+        slot = slots[s, j] + c
+        score, wgrad = scores.at[slot], wgrads.at[slot]
+        rows = pl.ds(c * HALF + low, high - low)
         keyed = jnp.concatenate([win[0, s, rows], key_doc[rows]], axis=1)
-        asked = jnp.concatenate([qo[0, s, c, j], query_doc[low:low + HALF]], axis=1)
-        score[...] = lax.dot_general(keyed, asked, NT, preferred_element_type=jnp.float32)
-        wgrad[...] = lax.dot_general(
+        asked = jnp.concatenate([qo[0, s, c, j], query_doc[c * HALF:(c + 1) * HALF]], axis=1)
+        score[low:high] = lax.dot_general(keyed, asked, NT, preferred_element_type=jnp.float32)
+        wgrad[low:high] = lax.dot_general(
             win[1, s, rows], qo[1, s, c, j], NT, preferred_element_type=jnp.float32)
-
-    def close_unit(s, c, j, slot):
-        low = c * HALF
-        score, wgrad = scores[slot], wgrads[slot]
-        score[REACH:SPAN] = jnp.where(causal, score[REACH:SPAN], -1e30)
+        if high == SPAN:
+            score[REACH:SPAN] = jnp.where(causal, score[REACH:SPAN], -1e30)
         peak = None
-        for t in tiles:
+        for t in range(low, high, TILE):
             x = score[t:t + TILE]
             x = jnp.max(x.reshape(TILE // 8, 8, HALF), axis=0)
             peak = x if peak is None else jnp.maximum(peak, x)
         top = jnp.max(peak, axis=0, keepdims=True)
         total = jnp.zeros((8, HALF), jnp.float32)
         dots = jnp.zeros((8, HALF), jnp.float32)
-        for t in tiles:
+        for t in range(low, high, TILE):
             e = jnp.exp2((score[t:t + TILE] - top) * (SCALE * LOG2E))
             score[t:t + TILE] = e
             total += fold(e)
             dots += fold(e * wgrad[t:t + TILE])
-        inverse = 1.0 / jnp.sum(total, axis=0, keepdims=True)
-        delta = jnp.sum(dots, axis=0, keepdims=True) * inverse
+        return top, jnp.sum(total, axis=0, keepdims=True), jnp.sum(dots, axis=0, keepdims=True)
+
+    def early(s, c, j):
+        slot = slots[s, j] + c
+        for row, value in enumerate(part(s, c, j, TOK - c * HALF, SPAN)):
+            stats[slot, row:row + 1] = value
+
+    def late(s, c, j):
+        slot, border = slots[s, j] + c, TOK - c * HALF
+        score, wgrad = scores.at[slot], wgrads.at[slot]
+        far_top, far_total, far_dots = part(s, c, j, 0, border)
+        near_top, near_total, near_dots = (stats[slot, row:row + 1] for row in range(3))
+        top = jnp.maximum(far_top, near_top)
+        far_scale = jnp.exp2((far_top - top) * (SCALE * LOG2E))
+        near_scale = jnp.exp2((near_top - top) * (SCALE * LOG2E))
+        inverse = 1.0 / (far_total * far_scale + near_total * near_scale)
+        delta = (far_dots * far_scale + near_dots * near_scale) * inverse
         at = pl.ds(c * TOK + j * HALF, HALF)
-        for t in tiles:
-            weights = score[t:t + TILE] * inverse
-            pd[s, 1, low + t:low + t + TILE, at] = weights.astype(jnp.bfloat16)
-            pd[s, 0, low + t:low + t + TILE, at] = (weights * (wgrad[t:t + TILE] - delta)).astype(jnp.bfloat16)
+        for t in range(0, SPAN, TILE):
+            weights = score[t:t + TILE] * ((far_scale if t < border else near_scale) * inverse)
+            rows = slice(c * HALF + t, c * HALF + t + TILE)
+            pd[s, 1, rows, at] = weights.astype(jnp.bfloat16)
+            pd[s, 0, rows, at] = (weights * (wgrad[t:t + TILE] - delta)).astype(jnp.bfloat16)
 
     def query_grads(s):
         for c in halves:
@@ -308,47 +320,58 @@
         m2[s].start()
 
     forward(0)
+    m1_in[0].wait_recv()
+    early(0, 0, 0)
+    early(0, 1, 0)
 
     @pl.when(jnp.logical_not(at_start))
     def _():
         forward(1)
 
     pass_on(0)
-    arrive(0)
-    m1_in[0].wait_recv()
-    m2_in[0].wait_recv()
-    open_unit(0, 0, 0, 0)
-    open_unit(0, 1, 0, 1)
-    close_unit(0, 0, 0, 0)
-
-    @pl.when(at_start)
-    def _():
-        forward(1)
+
+    @pl.when(jnp.logical_not(at_start))
+    def _():
+        m1_in[1].wait_recv()
+        early(1, 0, 0)
+        early(1, 1, 0)
 
     for copy in xq[0]:
         copy.wait_recv()
-    open_unit(0, 0, 1, 0)
-    close_unit(0, 1, 0, 1)
+    early(0, 0, 1)
+    arrive(0)
+    early(0, 1, 1)
+    m2_in[0].wait_recv()
+    late(0, 0, 0)
+
+    @pl.when(at_start)
+    def _():
+        forward(1)
+
+    late(0, 1, 0)
     pass_on(1)
-    open_unit(0, 1, 1, 1)
-    close_unit(0, 0, 1, 0)
-    close_unit(0, 1, 1, 1)
+    late(0, 0, 1)
+    late(0, 1, 1)
     outer(0)
-    arrive(1)
-    query_grads(0)
-    m1_in[1].wait_recv()
-    m2_in[1].wait_recv()
-    open_unit(1, 0, 0, 0)
-    open_unit(1, 1, 0, 1)
-    close_unit(1, 0, 0, 0)
+
+    @pl.when(at_start)
+    def _():
+        m1_in[1].wait_recv()
+        early(1, 0, 0)
+        early(1, 1, 0)
+
     for copy in xq[1]:
         copy.wait_recv()
-    open_unit(1, 0, 1, 0)
-    close_unit(1, 1, 0, 1)
+    early(1, 0, 1)
+    arrive(1)
+    early(1, 1, 1)
+    query_grads(0)
+    m2_in[1].wait_recv()
+    late(1, 0, 0)
+    late(1, 1, 0)
     middle(0)
-    open_unit(1, 1, 1, 1)
-    close_unit(1, 0, 1, 0)
-    close_unit(1, 1, 1, 1)
+    late(1, 0, 1)
+    late(1, 1, 1)
     outer(1)
     query_grads(1)
     middle(1)
@@ -378,7 +401,6 @@
     quad = pltpu.SemaphoreType.DMA((STAGES, 2))
     eight = pltpu.SemaphoreType.DMA((STAGES, 4))
     block16 = pltpu.VMEM((STAGES, TOK, HD), bf16)
-    unit32 = pltpu.VMEM((SPAN, HALF), f32)
     heads16 = pltpu.VMEM((STAGES, 4, 128, HD), bf16)
     dq, dk, dv = pl.pallas_call(
         lambda *refs: kernel(ctx_size, *refs),
@@ -393,7 +415,9 @@
             pltpu.VMEM((2, STAGES, WIN, HD), bf16),
             pltpu.VMEM((2, STAGES, 2, 2, HALF, HD), bf16),
             pltpu.VMEM((STAGES, 2, WIN, 2 * TOK), bf16),
-            unit32, unit32, unit32, unit32,
+            pltpu.VMEM((6, SPAN, HALF), f32),
+            pltpu.VMEM((6, SPAN, HALF), f32),
+            pltpu.VMEM((6, 8, HALF), f32),
             pltpu.VMEM((WIN, HD), f32),
             pltpu.VMEM((STAGES, 2, 2, HALF, HD), bf16),
             pltpu.VMEM((WIN, HD), bf16),

time: 53.8 us -> 53 us (0.985)
  Pallas kernels: 50.9 us -> 50.1 us
    pallas_call x1, Pallas kernels: 50.9 us -> 50.1 us  [local(): pl.pallas_call(lambda *refs: kernel(ctx_size, *refs), out_shape=(pltpu.VM...]
where the time goes in v4:
time: 53 us; the launch traced here: 52.9 us
  Pallas kernels  50.1 us (95%)
  local copies, waits for them, and re-layouts  2.11 us (4%)
  between operations  0.64 us (1%)
    pallas_call x1, Pallas kernels, local(): pl.pallas_call(lambda *refs: kernel(ctx_size, *refs), out_shape=(pltpu.VM...  50.1 us
    unnamed x3, local copies, waits for them, and re-layouts  2.11 us

profile of v4, /device:TPU:1, one launch (start us, length us, event | category | flops | bytes accessed | tf_op | source)
XLA Modules:
  0.0 52.9 jit_solution(14259763362653000675)
XLA Ops:
  0.6 50.1 %attention_backward.1 = (bf16[2,256,512]{2,1,0:T(8,128)(2,1)S(1)}, bf16[128,512]{1,0:T(8,128)(2,1)S(1)}, bf16[128,512]{1,0:T(8,128)(2,1)S(1)}) custom-call(bf16[2,256,512]{2,1,0:T(8,128)(2,1)} %bitcast.5, bf16[512,512]{1,0:T(8,128)(2,1)} %refs_1_.1, bf16[512,512]{1,0:T(8,128)(2,1)} %refs_2_.1, bf16[2,256,512]{2,1,0:T(8,128)(2,1)} %bitcast.6, s32[1,64]{1,0:T(1,128)} %bitcast.7), custom_call_target="tpu_custom_call" | custom-call | flops 3355443200 | bytes 4194304 | tf_op jit(solution)/shard_map/attention_backward/pallas_call | solution.py:405
  50.8 0.8 %copy.11 = bf16[512,1,512]{2,0,1:T(8,128)(2,1)} copy(bf16[512,1,512]{2,0,1:T(8,128)(2,1)S(1)} %bitcast.4) | data formatting | bytes 1048576
  51.6 0.7 %copy.12 = bf16[128,512]{1,0:T(8,128)(2,1)} copy(bf16[128,512]{1,0:T(8,128)(2,1)S(1)} %get-tuple-element.10) | data formatting | bytes 262144
  52.2 0.7 %copy.13 = bf16[128,512]{1,0:T(8,128)(2,1)} copy(bf16[128,512]{1,0:T(8,128)(2,1)S(1)} %get-tuple-element.11) | data formatting | bytes 262144

commit v5 on v4

--- a/solution.py
+++ b/solution.py
@@ -146,8 +146,14 @@
             direct.start()
 
     either(z1[1], z1_relayed)
-    for copy in (*xq[0], *xq[1]):
+    for copy in xq[0]:
         copy.start()
+
+    @pl.when(jnp.logical_not(at_start | at_end))
+    def _():
+        for copy in xq[1]:
+            copy.start()
+
 
     lengths = len_ref[...]
     upto = jnp.where(
@@ -338,6 +344,12 @@
 
     for copy in xq[0]:
         copy.wait_recv()
+
+    @pl.when(at_start | at_end)
+    def _():
+        for copy in xq[1]:
+            copy.start()
+
     early(0, 0, 1)
     arrive(0)
     early(0, 1, 1)
@@ -392,6 +404,16 @@
                 h0[s][q].wait_send()
         dq_far_in[s].wait_recv()
         dq_near[s].wait()
+
+
+def write_out(*refs):
+    sources, targets, sem = refs[0:3], refs[3:6], refs[6]
+    copies = [pltpu.make_async_copy(source, target, sem.at[i])
+              for i, (source, target) in enumerate(zip(sources, targets, strict=True))]
+    for copy in copies:
+        copy.start()
+    for copy in copies:
+        copy.wait()
 
 
 def local(ctx_size, queries, keys, values, grad_out, doc_lengths):
@@ -441,6 +463,15 @@
         name="attention_backward",
     )(queries.reshape(2, HALF, KVH * HD), keys, values, grad_out.reshape(2, HALF, KVH * HD),
       doc_lengths.reshape(1, 64))
+    dq, dk, dv = pl.pallas_call(
+        write_out,
+        out_shape=tuple(jax.ShapeDtypeStruct(x.shape, bf16) for x in (dq, dk, dv)),
+        in_specs=[anywhere] * 3,
+        out_specs=(anywhere,) * 3,
+        scratch_shapes=[pltpu.SemaphoreType.DMA((3,))],
+        compiler_params=pltpu.CompilerParams(vmem_limit_bytes=4 * 2**20),
+        name="write_out",
+    )(dq, dk, dv)
     return dq.reshape(TOK, 1, KVH * HD), dk, dv
 
 

time: 53 us -> 51.7 us (0.975)
  local copies, waits for them, and re-layouts: 2.11 us -> 0 us
  Pallas kernels: 50.1 us -> 50.7 us
    unnamed x3 -> x0, local copies, waits for them, and re-layouts: 2.11 us -> none
    pallas_call x0 -> x1, Pallas kernels: none -> 0.9 us  [local(): pl.pallas_call(write_out, out_shape=tuple((jax.ShapeDtypeStruct(x.shape,...]
where the time goes in v5:
time: 51.7 us; the launch traced here: 51.5 us
  Pallas kernels  50.7 us (98%)
  between operations  0.8 us (2%)
    pallas_call x1, Pallas kernels, local(): pl.pallas_call(lambda *refs: kernel(ctx_size, *refs), out_shape=(pltpu.VM...  49.8 us

profile of v5, /device:TPU:1, one launch (start us, length us, event | category | flops | bytes accessed | tf_op | source)
XLA Modules:
  0.0 51.5 jit_solution(2836177990723956568)
XLA Ops:
  0.6 49.8 %attention_backward.1 = (bf16[2,256,512]{2,1,0:T(8,128)(2,1)S(1)}, bf16[128,512]{1,0:T(8,128)(2,1)S(1)}, bf16[128,512]{1,0:T(8,128)(2,1)S(1)}) custom-call(bf16[2,256,512]{2,1,0:T(8,128)(2,1)} %bitcast.4, bf16[512,512]{1,0:T(8,128)(2,1)} %refs_1_.1, bf16[512,512]{1,0:T(8,128)(2,1)} %refs_2_.1, bf16[2,256,512]{2,1,0:T(8,128)(2,1)} %bitcast.5, s32[1,64]{1,0:T(1,128)} %bitcast.7), custom_call_target="tpu_custom_call" | custom-call | flops 3355443200 | bytes 4194304 | tf_op jit(solution)/shard_map/attention_backward/pallas_call | solution.py:427
  50.5 0.9 %write_out.1 = (bf16[2,256,512]{2,1,0:T(8,128)(2,1)}, bf16[128,512]{1,0:T(8,128)(2,1)}, bf16[128,512]{1,0:T(8,128)(2,1)}) custom-call(bf16[2,256,512]{2,1,0:T(8,128)(2,1)S(1)} %get-tuple-element.9.refs_0_, bf16[128,512]{1,0:T(8,128)(2,1)S(1)} %get-tuple-element.10.refs_1_, bf16[128,512]{1,0:T(8,128)(2,1)S(1)} %get-tuple-element.11.refs_2_), custom_call_target="tpu_custom_call" | custom-call | tf_op jit(solution)/shard_map/write_out/pallas_call | solution.py:466

commit v6 on v5

--- a/solution.py
+++ b/solution.py
@@ -372,17 +372,17 @@
         early(1, 0, 0)
         early(1, 1, 0)
 
-    for copy in xq[1]:
-        copy.wait_recv()
-    early(1, 0, 1)
     arrive(1)
-    early(1, 1, 1)
     query_grads(0)
     m2_in[1].wait_recv()
     late(1, 0, 0)
     late(1, 1, 0)
     middle(0)
+    for copy in xq[1]:
+        copy.wait_recv()
+    early(1, 0, 1)
     late(1, 0, 1)
+    early(1, 1, 1)
     late(1, 1, 1)
     outer(1)
     query_grads(1)

time: 51.7 us -> 50.8 us (0.983)
  Pallas kernels: 50.7 us -> 49.8 us
    pallas_call x1, Pallas kernels: 49.8 us -> 48.9 us  [local(): pl.pallas_call(lambda *refs: kernel(ctx_size, *refs), out_shape=(pltpu.VM...]
where the time goes in v6:
time: 50.8 us; the launch traced here: 50.6 us
  Pallas kernels  49.8 us (98%)
  between operations  0.8 us (2%)
    pallas_call x1, Pallas kernels, local(): pl.pallas_call(lambda *refs: kernel(ctx_size, *refs), out_shape=(pltpu.VM...  48.9 us

profile of v6, /device:TPU:1, one launch (start us, length us, event | category | flops | bytes accessed | tf_op | source)
XLA Modules:
  0.0 50.6 jit_solution(911619943025874904)
XLA Ops:
  0.6 48.9 %attention_backward.1 = (bf16[2,256,512]{2,1,0:T(8,128)(2,1)S(1)}, bf16[128,512]{1,0:T(8,128)(2,1)S(1)}, bf16[128,512]{1,0:T(8,128)(2,1)S(1)}) custom-call(bf16[2,256,512]{2,1,0:T(8,128)(2,1)} %bitcast.4, bf16[512,512]{1,0:T(8,128)(2,1)} %refs_1_.1, bf16[512,512]{1,0:T(8,128)(2,1)} %refs_2_.1, bf16[2,256,512]{2,1,0:T(8,128)(2,1)} %bitcast.5, s32[1,64]{1,0:T(1,128)} %bitcast.7), custom_call_target="tpu_custom_call" | custom-call | flops 3355443200 | bytes 4194304 | tf_op jit(solution)/shard_map/attention_backward/pallas_call | solution.py:427
  49.6 0.9 %write_out.1 = (bf16[2,256,512]{2,1,0:T(8,128)(2,1)}, bf16[128,512]{1,0:T(8,128)(2,1)}, bf16[128,512]{1,0:T(8,128)(2,1)}) custom-call(bf16[2,256,512]{2,1,0:T(8,128)(2,1)S(1)} %get-tuple-element.9.refs_0_, bf16[128,512]{1,0:T(8,128)(2,1)S(1)} %get-tuple-element.10.refs_1_, bf16[128,512]{1,0:T(8,128)(2,1)S(1)} %get-tuple-element.11.refs_2_), custom_call_target="tpu_custom_call" | custom-call | tf_op jit(solution)/shard_map/write_out/pallas_call | solution.py:466

commit v7 on v6

--- a/solution.py
+++ b/solution.py
@@ -360,8 +360,8 @@
     def _():
         forward(1)
 
+    pass_on(1)
     late(0, 1, 0)
-    pass_on(1)
     late(0, 0, 1)
     late(0, 1, 1)
     outer(0)

time: 50.8 us -> 50.4 us (level)
  no operation moved by 1% of the time
where the time goes in v7:
time: 50.4 us; the launch traced here: 50.3 us
  Pallas kernels  49.5 us (98%)
  between operations  0.8 us (2%)
    pallas_call x1, Pallas kernels, local(): pl.pallas_call(lambda *refs: kernel(ctx_size, *refs), out_shape=(pltpu.VM...  48.6 us

profile of v7, /device:TPU:1, one launch (start us, length us, event | category | flops | bytes accessed | tf_op | source)
XLA Modules:
  0.0 50.3 jit_solution(1105427057453310398)
XLA Ops:
  0.6 48.6 %attention_backward.1 = (bf16[2,256,512]{2,1,0:T(8,128)(2,1)S(1)}, bf16[128,512]{1,0:T(8,128)(2,1)S(1)}, bf16[128,512]{1,0:T(8,128)(2,1)S(1)}) custom-call(bf16[2,256,512]{2,1,0:T(8,128)(2,1)} %bitcast.4, bf16[512,512]{1,0:T(8,128)(2,1)} %refs_1_.1, bf16[512,512]{1,0:T(8,128)(2,1)} %refs_2_.1, bf16[2,256,512]{2,1,0:T(8,128)(2,1)} %bitcast.5, s32[1,64]{1,0:T(1,128)} %bitcast.7), custom_call_target="tpu_custom_call" | custom-call | flops 3355443200 | bytes 4194304 | tf_op jit(solution)/shard_map/attention_backward/pallas_call | solution.py:427
  49.2 0.9 %write_out.1 = (bf16[2,256,512]{2,1,0:T(8,128)(2,1)}, bf16[128,512]{1,0:T(8,128)(2,1)}, bf16[128,512]{1,0:T(8,128)(2,1)}) custom-call(bf16[2,256,512]{2,1,0:T(8,128)(2,1)S(1)} %get-tuple-element.9.refs_0_, bf16[128,512]{1,0:T(8,128)(2,1)S(1)} %get-tuple-element.10.refs_1_, bf16[128,512]{1,0:T(8,128)(2,1)S(1)} %get-tuple-element.11.refs_2_), custom_call_target="tpu_custom_call" | custom-call | tf_op jit(solution)/shard_map/write_out/pallas_call | solution.py:466

commit v8 on v7

--- a/solution.py
+++ b/solution.py
@@ -386,8 +386,8 @@
     late(1, 1, 1)
     outer(1)
     query_grads(1)
+    finish(0)
     middle(1)
-    finish(0)
     finish(1)
 
     @pl.when(at_end)

time: 50.4 us -> 50.4 us (level)
  no operation moved by 1% of the time
where the time goes in v8:
time: 50.4 us; the launch traced here: 50.3 us
  Pallas kernels  49.5 us (98%)
  between operations  0.8 us (2%)
    pallas_call x1, Pallas kernels, local(): pl.pallas_call(lambda *refs: kernel(ctx_size, *refs), out_shape=(pltpu.VM...  48.6 us

profile of v8, /device:TPU:1, one launch (start us, length us, event | category | flops | bytes accessed | tf_op | source)
XLA Modules:
  0.0 50.3 jit_solution(3741800510084649893)
XLA Ops:
  0.6 48.6 %attention_backward.1 = (bf16[2,256,512]{2,1,0:T(8,128)(2,1)S(1)}, bf16[128,512]{1,0:T(8,128)(2,1)S(1)}, bf16[128,512]{1,0:T(8,128)(2,1)S(1)}) custom-call(bf16[2,256,512]{2,1,0:T(8,128)(2,1)} %bitcast.4, bf16[512,512]{1,0:T(8,128)(2,1)} %refs_1_.1, bf16[512,512]{1,0:T(8,128)(2,1)} %refs_2_.1, bf16[2,256,512]{2,1,0:T(8,128)(2,1)} %bitcast.5, s32[1,64]{1,0:T(1,128)} %bitcast.7), custom_call_target="tpu_custom_call" | custom-call | flops 3355443200 | bytes 4194304 | tf_op jit(solution)/shard_map/attention_backward/pallas_call | solution.py:427
  49.2 0.9 %write_out.1 = (bf16[2,256,512]{2,1,0:T(8,128)(2,1)}, bf16[128,512]{1,0:T(8,128)(2,1)}, bf16[128,512]{1,0:T(8,128)(2,1)}) custom-call(bf16[2,256,512]{2,1,0:T(8,128)(2,1)S(1)} %get-tuple-element.9.refs_0_, bf16[128,512]{1,0:T(8,128)(2,1)S(1)} %get-tuple-element.10.refs_1_, bf16[128,512]{1,0:T(8,128)(2,1)S(1)} %get-tuple-element.11.refs_2_), custom_call_target="tpu_custom_call" | custom-call | tf_op jit(solution)/shard_map/write_out/pallas_call | solution.py:466
